TPU v7x, 32 devices: a whole 2x2x4 slice. The times are simulated.
32 devices in a mesh: grp: 2 (over x), gy: 4 (over y, core), gz: 4 (over z).
Axes of the slice: x: 2, y: 2, z: 4, core: 2. Of those that a mesh axis runs over, the one named last changes fastest.
Arguments:
- velocity: float32 [3, 32, 32, 256], P(None, 'gy', 'gz', 'grp'), may hold values from -5 to 5
- basis_old: bfloat16 [64, 3, 16, 16, 256], P(None, None, 'gy', 'gz', 'grp'), may hold values from -64 to 64
- strength: float32 [64], replicated, may hold values from 0.3 to 3
- snapshots: bfloat16 [63, 3, 16, 16, 256], P(None, None, 'gy', 'gz', 'grp'), may hold values from -64 to 64
Outputs:
- advanced: float32 [3, 32, 32, 256], P(None, 'gy', 'gz', 'grp')
- basis_new: bfloat16 [128, 3, 16, 16, 256], P(None, None, 'gy', 'gz', 'grp')
- root_factor: float32 [128, 128], replicated
All inputs are finite; a program needn't handle non-finite values.
Results may differ from a plain program's by a relative error of at most 0.0012.
The roundings to bfloat16 on the way count: a program that leaves them out, or rounds other values in their place, can miss the bound.
Values sent between devices are 32-bit elements; how exact they have to be, the bound alone decides.
A program may use at most 64 MiB of HBM per device.

v0:
```python
import jax
import jax.numpy as jnp
from jax import lax
from jax.sharding import PartitionSpec as P

NS_ITERS = 8


time_step = 0.1
viscosity = 0.05


def padded_2(block, sides, width):
    for axis, dim in sides:
        count = lax.axis_size(axis)
        forward = [(i, i + 1) for i in range(count - 1)]
        forward.append((count - 1, 0))
        backward = [(target, source) for source, target in forward]
        low = lax.ppermute(
            lax.slice_in_dim(block, block.shape[dim] - width, None, axis=dim), axis, forward
        )
        high = lax.ppermute(lax.slice_in_dim(block, 0, width, axis=dim), axis, backward)
        block = jnp.concatenate([low, block, high], axis=dim)
    return block


def tendency(padded, field):
    y_plus = padded[:, 2:, 1:-1, 1:-1]
    y_minus = padded[:, :-2, 1:-1, 1:-1]
    z_plus = padded[:, 1:-1, 2:, 1:-1]
    z_minus = padded[:, 1:-1, :-2, 1:-1]
    x_plus = padded[:, 1:-1, 1:-1, 2:]
    x_minus = padded[:, 1:-1, 1:-1, :-2]
    carried = field[0][None] * (x_plus - x_minus) * 0.5
    carried = carried + field[1][None] * (y_plus - y_minus) * 0.5
    carried = carried + field[2][None] * (z_plus - z_minus) * 0.5
    spread = x_plus + x_minus + y_plus + y_minus + z_plus + z_minus - 6.0 * field
    return viscosity * spread - carried


def faces(field):
    padded = padded_2(field, (("grp", 3), ("gy", 1), ("gz", 2)), 1)
    position = lax.axis_index("gy")
    bottom = jnp.where(position == 0, 0.0, padded[:, 0, :, :])
    upper = jnp.where(position == lax.axis_size("gy") - 1, 0.0, padded[:, -1, :, :])
    return padded.at[:, 0, :, :].set(bottom).at[:, -1, :, :].set(upper)


def advance(field):
    for repeat in range(2):
        first = field + time_step * tendency(faces(field), field)
        second = 0.75 * field + 0.25 * (first + time_step * tendency(faces(first), first))
        field = field / 3.0 + 2.0 / 3.0 * (second + time_step * tendency(faces(second), second))
    return field


def local(velocity, basis_old, strength, snapshots):
    modes = basis_old.shape[0]
    earlier_count = snapshots.shape[0]
    head = (strength[:, None] * basis_old.reshape(modes, -1).astype(jnp.float32)).astype(
        jnp.bfloat16
    )
    earlier = jnp.concatenate([head, snapshots.reshape(earlier_count, -1)], axis=0)
    old_sum = lax.psum(
        jnp.dot(earlier, earlier.T, preferred_element_type=jnp.float32), ("grp", "gy", "gz")
    )
    field = advance(velocity)
    newest = field[:, ::2, ::2, :].reshape(1, -1).astype(jnp.bfloat16)
    whole = jnp.concatenate([earlier, newest], axis=0)
    cross = lax.psum(
        jnp.dot(whole, newest[0], preferred_element_type=jnp.float32), ("grp", "gy", "gz")
    )
    upper_rows = jnp.concatenate([old_sum, cross[:-1, None]], axis=1)
    gram = jnp.concatenate([upper_rows, cross[None, :]], axis=0)
    ranks = whole.shape[0]
    scale = jnp.sqrt(jnp.sum(gram * gram))
    level = gram / scale
    ident = jnp.eye(ranks, dtype=jnp.float32)
    inverse = ident
    for repeat in range(NS_ITERS):
        factor = 1.5 * ident - 0.5 * jnp.dot(inverse, level, precision=lax.Precision.HIGHEST)
        level = jnp.dot(level, factor, precision=lax.Precision.HIGHEST)
        inverse = jnp.dot(factor, inverse, precision=lax.Precision.HIGHEST)
    total_rows = whole.shape[1] * lax.axis_size("grp") * lax.axis_size("gy") * lax.axis_size("gz")
    weights = (inverse * (jnp.sqrt(jnp.float32(total_rows)) / jnp.sqrt(scale))).astype(jnp.bfloat16)
    basis_new = jnp.dot(weights, whole, preferred_element_type=jnp.float32).astype(jnp.bfloat16)
    basis_new = basis_new.reshape(
        ranks, 3, field.shape[1] // 2, field.shape[2] // 2, field.shape[3]
    )
    return (field, basis_new, level)


def solution(mesh):
    placed = (
        P(None, "gy", "gz", "grp"),
        P(None, None, "gy", "gz", "grp"),
        P(),
        P(None, None, "gy", "gz", "grp"),
    )
    return jax.shard_map(
        local,
        mesh=mesh,
        in_specs=placed,
        out_specs=(P(None, "gy", "gz", "grp"), P(None, None, "gy", "gz", "grp"), P()),
        check_vma=False,
    )
```

profile of v0, /device:TPU:0, one launch (start us, length us, event | category | flops | bytes accessed | tf_op | source)
XLA Modules:
  0.0 160.9 jit_solution(7566356806122562326)
XLA Ops:
  1.7 3.0 %collective-permute-start = (f32[3,8,8,1]{3,2,1,0:T(8,128)S(1)}, f32[3,8,8,1]{3,2,1,0:T(8,128)S(1)}, u32[]{:S(2)}, u32[]{:S(2)}) collective-permute-start(f32[3,8,8,1]{3,2,1,0:T(8,128)S(1)} %get-tuple-element.203), channel_id=1, source_target_pairs={{0,16},{16,0},{1,17},{17,1},{2,18},{18,2},{3,19},{19,3},{4,20},{20... | collective-permute-start | bytes 2312 | tf_op jit(solution)/shard_map/ppermute | solution.py:19
  4.8 3.4 %collective-permute-done = f32[3,8,8,1]{3,2,1,0:T(8,128)S(1)} collective-permute-done((f32[3,8,8,1]{3,2,1,0:T(8,128)S(1)}, f32[3,8,8,1]{3,2,1,0:T(8,128)S(1)}, u32[]{:S(2)}, u32[]{:S(2)}) %collective-permute-start) | collective-permute-done | bytes 800 | tf_op jit(solution)/shard_map/ppermute | solution.py:19
  14.9 2.0 %collective-permute-start.4 = (f32[3,10,1,130]{3,2,1,0:T(1,128)S(1)}, f32[3,10,1,130]{3,2,1,0:T(1,128)S(1)}, u32[]{:S(2)}, u32[]{:S(2)}) collective-permute-start(f32[3,10,1,130]{3,2,1,0:T(1,128)S(1)} %get-tuple-element.161), channel_id=1, source_target_pairs={{0,1},{1,2},{2,3},{3,0},{4,5},{5,6},{6,7},{7,4},{8,9},{9,10},{10,1... | collective-permute-start | bytes 46808 | tf_op jit(solution)/shard_map/ppermute | solution.py:19
  16.9 2.1 %collective-permute-start.5 = (f32[3,10,1,130]{3,2,1,0:T(1,128)S(1)}, f32[3,10,1,130]{3,2,1,0:T(1,128)S(1)}, u32[]{:S(2)}, u32[]{:S(2)}) collective-permute-start(f32[3,10,1,130]{3,2,1,0:T(1,128)S(1)} %get-tuple-element.162), channel_id=1, source_target_pairs={{1,0},{2,1},{3,2},{0,3},{5,4},{6,5},{7,6},{4,7},{9,8},{10,9},{11,1... | collective-permute-start | bytes 46808 | tf_op jit(solution)/shard_map/ppermute | solution.py:22
  24.9 3.6 %collective-permute-done.6 = f32[3,8,8,1]{3,2,1,0:T(8,128)S(1)} collective-permute-done((f32[3,8,8,1]{3,2,1,0:T(8,128)S(1)}, f32[3,8,8,1]{3,2,1,0:T(8,128)S(1)}, u32[]{:S(2)}, u32[]{:S(2)}) %collective-permute-start.6) | collective-permute-done | bytes 800 | tf_op jit(solution)/shard_map/ppermute | solution.py:19
  35.0 2.5 %collective-permute-start.11 = (f32[3,10,1,130]{3,2,1,0:T(1,128)S(1)}, f32[3,10,1,130]{3,2,1,0:T(1,128)S(1)}, u32[]{:S(2)}, u32[]{:S(2)}) collective-permute-start(f32[3,10,1,130]{3,2,1,0:T(1,128)S(1)} %get-tuple-element.160), channel_id=1, source_target_pairs={{1,0},{2,1},{3,2},{0,3},{5,4},{6,5},{7,6},{4,7},{9,8},{10,9},{11,1... | collective-permute-start | bytes 46808 | tf_op jit(solution)/shard_map/ppermute | solution.py:22
  37.5 2.2 %collective-permute-done.10 = f32[3,10,1,130]{3,2,1,0:T(1,128)S(1)} collective-permute-done((f32[3,10,1,130]{3,2,1,0:T(1,128)S(1)}, f32[3,10,1,130]{3,2,1,0:T(1,128)S(1)}, u32[]{:S(2)}, u32[]{:S(2)}) %collective-permute-start.10) | collective-permute-done | bytes 15632 | tf_op jit(solution)/shard_map/ppermute | solution.py:19
  42.4 3.6 %collective-permute-done.12 = f32[3,8,8,1]{3,2,1,0:T(8,128)S(1)} collective-permute-done((f32[3,8,8,1]{3,2,1,0:T(8,128)S(1)}, f32[3,8,8,1]{3,2,1,0:T(8,128)S(1)}, u32[]{:S(2)}, u32[]{:S(2)}) %collective-permute-start.12) | collective-permute-done | bytes 800 | tf_op jit(solution)/shard_map/ppermute | solution.py:19
  52.1 2.6 %collective-permute-start.17 = (f32[3,10,1,130]{3,2,1,0:T(1,128)S(1)}, f32[3,10,1,130]{3,2,1,0:T(1,128)S(1)}, u32[]{:S(2)}, u32[]{:S(2)}) collective-permute-start(f32[3,10,1,130]{3,2,1,0:T(1,128)S(1)} %get-tuple-element.158), channel_id=1, source_target_pairs={{1,0},{2,1},{3,2},{0,3},{5,4},{6,5},{7,6},{4,7},{9,8},{10,9},{11,1... | collective-permute-start | bytes 46808 | tf_op jit(solution)/shard_map/ppermute | solution.py:22
  54.8 2.0 %collective-permute-done.16 = f32[3,10,1,130]{3,2,1,0:T(1,128)S(1)} collective-permute-done((f32[3,10,1,130]{3,2,1,0:T(1,128)S(1)}, f32[3,10,1,130]{3,2,1,0:T(1,128)S(1)}, u32[]{:S(2)}, u32[]{:S(2)}) %collective-permute-start.16) | collective-permute-done | bytes 15632 | tf_op jit(solution)/shard_map/ppermute | solution.py:19
  59.5 3.6 %collective-permute-done.18 = f32[3,8,8,1]{3,2,1,0:T(8,128)S(1)} collective-permute-done((f32[3,8,8,1]{3,2,1,0:T(8,128)S(1)}, f32[3,8,8,1]{3,2,1,0:T(8,128)S(1)}, u32[]{:S(2)}, u32[]{:S(2)}) %collective-permute-start.18) | collective-permute-done | bytes 800 | tf_op jit(solution)/shard_map/ppermute | solution.py:19
  64.5 1.7 %collective-permute-start.21 = (f32[3,1,8,130]{3,2,1,0:T(8,128)S(1)}, f32[3,1,8,130]{3,2,1,0:T(8,128)S(1)}, u32[]{:S(2)}, u32[]{:S(2)}) collective-permute-start(f32[3,1,8,130]{3,2,1,0:T(8,128)S(1)} %get-tuple-element.168), channel_id=1, source_target_pairs={{4,0},{8,4},{12,8},{0,12},{5,1},{9,5},{13,9},{1,13},{6,2},{10,6},{... | collective-permute-start | bytes 37448 | tf_op jit(solution)/shard_map/ppermute | solution.py:22
  69.4 2.7 %collective-permute-start.23 = (f32[3,10,1,130]{3,2,1,0:T(1,128)S(1)}, f32[3,10,1,130]{3,2,1,0:T(1,128)S(1)}, u32[]{:S(2)}, u32[]{:S(2)}) collective-permute-start(f32[3,10,1,130]{3,2,1,0:T(1,128)S(1)} %get-tuple-element.156), channel_id=1, source_target_pairs={{1,0},{2,1},{3,2},{0,3},{5,4},{6,5},{7,6},{4,7},{9,8},{10,9},{11,1... | collective-permute-start | bytes 46808 | tf_op jit(solution)/shard_map/ppermute | solution.py:22
  72.1 1.9 %collective-permute-done.22 = f32[3,10,1,130]{3,2,1,0:T(1,128)S(1)} collective-permute-done((f32[3,10,1,130]{3,2,1,0:T(1,128)S(1)}, f32[3,10,1,130]{3,2,1,0:T(1,128)S(1)}, u32[]{:S(2)}, u32[]{:S(2)}) %collective-permute-start.22) | collective-permute-done | bytes 15632 | tf_op jit(solution)/shard_map/ppermute | solution.py:19
  76.6 3.6 %collective-permute-done.24 = f32[3,8,8,1]{3,2,1,0:T(8,128)S(1)} collective-permute-done((f32[3,8,8,1]{3,2,1,0:T(8,128)S(1)}, f32[3,8,8,1]{3,2,1,0:T(8,128)S(1)}, u32[]{:S(2)}, u32[]{:S(2)}) %collective-permute-start.24) | collective-permute-done | bytes 800 | tf_op jit(solution)/shard_map/ppermute | solution.py:19
  81.7 1.7 %collective-permute-start.27 = (f32[3,1,8,130]{3,2,1,0:T(8,128)S(1)}, f32[3,1,8,130]{3,2,1,0:T(8,128)S(1)}, u32[]{:S(2)}, u32[]{:S(2)}) collective-permute-start(f32[3,1,8,130]{3,2,1,0:T(8,128)S(1)} %get-tuple-element.166), channel_id=1, source_target_pairs={{4,0},{8,4},{12,8},{0,12},{5,1},{9,5},{13,9},{1,13},{6,2},{10,6},{... | collective-permute-start | bytes 37448 | tf_op jit(solution)/shard_map/ppermute | solution.py:22
  86.7 2.7 %collective-permute-start.29 = (f32[3,10,1,130]{3,2,1,0:T(1,128)S(1)}, f32[3,10,1,130]{3,2,1,0:T(1,128)S(1)}, u32[]{:S(2)}, u32[]{:S(2)}) collective-permute-start(f32[3,10,1,130]{3,2,1,0:T(1,128)S(1)} %get-tuple-element.154), channel_id=1, source_target_pairs={{1,0},{2,1},{3,2},{0,3},{5,4},{6,5},{7,6},{4,7},{9,8},{10,9},{11,1... | collective-permute-start | bytes 46808 | tf_op jit(solution)/shard_map/ppermute | solution.py:22
  89.4 2.1 %collective-permute-done.28 = f32[3,10,1,130]{3,2,1,0:T(1,128)S(1)} collective-permute-done((f32[3,10,1,130]{3,2,1,0:T(1,128)S(1)}, f32[3,10,1,130]{3,2,1,0:T(1,128)S(1)}, u32[]{:S(2)}, u32[]{:S(2)}) %collective-permute-start.28) | collective-permute-done | bytes 15632 | tf_op jit(solution)/shard_map/ppermute | solution.py:19
  95.0 1.7 %reshape.420 = bf16[63,6144]{1,0:T(8,128)(2,1)S(1)} reshape(bf16[63,3,4,4,128]{4,3,2,1,0:T(4,128)(2,1)} %param.31) | data formatting | bytes 1548288 | tf_op jit(solution)/shard_map/reshape | solution.py:63
  96.8 1.9 %collective-permute-done.30 = f32[3,8,8,1]{3,2,1,0:T(8,128)S(1)} collective-permute-done((f32[3,8,8,1]{3,2,1,0:T(8,128)}, f32[3,8,8,1]{3,2,1,0:T(8,128)S(1)}, u32[]{:S(2)}, u32[]{:S(2)}) %collective-permute-start.30) | collective-permute-done | bytes 800 | tf_op jit(solution)/shard_map/ppermute | solution.py:19
  104.8 2.6 %collective-permute-start.35 = (f32[3,10,1,130]{3,2,1,0:T(1,128)S(1)}, f32[3,10,1,130]{3,2,1,0:T(1,128)S(1)}, u32[]{:S(2)}, u32[]{:S(2)}) collective-permute-start(f32[3,10,1,130]{3,2,1,0:T(1,128)S(1)} %get-tuple-element.152), channel_id=1, source_target_pairs={{1,0},{2,1},{3,2},{0,3},{5,4},{6,5},{7,6},{4,7},{9,8},{10,9},{11,1... | collective-permute-start | bytes 46808 | tf_op jit(solution)/shard_map/ppermute | solution.py:22
  107.5 2.2 %collective-permute-done.34 = f32[3,10,1,130]{3,2,1,0:T(1,128)S(1)} collective-permute-done((f32[3,10,1,130]{3,2,1,0:T(1,128)S(1)}, f32[3,10,1,130]{3,2,1,0:T(1,128)S(1)}, u32[]{:S(2)}, u32[]{:S(2)}) %collective-permute-start.34) | collective-permute-done | bytes 15632 | tf_op jit(solution)/shard_map/ppermute | solution.py:19
  111.1 40.0 %all-reduce = (f32[128]{0:T(128)S(1)}, f32[127,127]{1,0:T(8,128)S(1)}) all-reduce(f32[128]{0:T(128)S(1)} %convolution_bitcast_fusion, f32[127,127]{1,0:T(8,128)S(1)} %fusion), channel_id=1, replica_groups=mesh['grp'=2,'gy'=4,'gz'=4] {'grp','gy','gz'}, use_global_device_ids=true, to_apply=%region_1.2 | all-reduce | flops 16257 | bytes 130056 | tf_op jit(solution)/shard_map/psum | solution.py:70
  158.9 2.0 %reshape.421 = bf16[128,3,4,4,128]{4,3,2,1,0:T(4,128)(2,1)} reshape(bf16[128,6144]{1,0:T(8,128)(2,1)S(1)} %convolution_convert_fusion) | data formatting | bytes 3145728 | tf_op jit(solution)/shard_map/reshape | solution.py:87
  (148 shorter events, 61.2 us)
Async XLA Ops:
  1.7 6.5 %collective-permute-start = (f32[3,8,8,1]{3,2,1,0:T(8,128)S(1)}, f32[3,8,8,1]{3,2,1,0:T(8,128)S(1)}, u32[]{:S(2)}, u32[]{:S(2)}) collective-permute-start(f32[3,8,8,1]{3,2,1,0:T(8,128)S(1)} %get-tuple-element.203), channel_id=1, source_target_pairs={{0,16},{16,0},{1,17},{17,1},{2,18},{18,2},{3,19},{19,3},{4,20},{20... | collective-permute-start | bytes 2312 | tf_op jit(solution)/shard_map/ppermute | solution.py:19
  4.7 4.9 %collective-permute-start.1 = (f32[3,8,8,1]{3,2,1,0:T(8,128)S(1)}, f32[3,8,8,1]{3,2,1,0:T(8,128)S(1)}, u32[]{:S(2)}, u32[]{:S(2)}) collective-permute-start(f32[3,8,8,1]{3,2,1,0:T(8,128)S(1)} %get-tuple-element.204), channel_id=1, source_target_pairs={{16,0},{0,16},{17,1},{1,17},{18,2},{2,18},{19,3},{3,19},{20,4},{4,... | collective-permute-start | bytes 2312 | tf_op jit(solution)/shard_map/ppermute | solution.py:22
  14.9 6.0 %collective-permute-start.4 = (f32[3,10,1,130]{3,2,1,0:T(1,128)S(1)}, f32[3,10,1,130]{3,2,1,0:T(1,128)S(1)}, u32[]{:S(2)}, u32[]{:S(2)}) collective-permute-start(f32[3,10,1,130]{3,2,1,0:T(1,128)S(1)} %get-tuple-element.161), channel_id=1, source_target_pairs={{0,1},{1,2},{2,3},{3,0},{4,5},{5,6},{6,7},{7,4},{8,9},{9,10},{10,1... | collective-permute-start | bytes 46808 | tf_op jit(solution)/shard_map/ppermute | solution.py:19
  16.9 4.4 %collective-permute-start.5 = (f32[3,10,1,130]{3,2,1,0:T(1,128)S(1)}, f32[3,10,1,130]{3,2,1,0:T(1,128)S(1)}, u32[]{:S(2)}, u32[]{:S(2)}) collective-permute-start(f32[3,10,1,130]{3,2,1,0:T(1,128)S(1)} %get-tuple-element.162), channel_id=1, source_target_pairs={{1,0},{2,1},{3,2},{0,3},{5,4},{6,5},{7,6},{4,7},{9,8},{10,9},{11,1... | collective-permute-start | bytes 46808 | tf_op jit(solution)/shard_map/ppermute | solution.py:22
  22.8 5.7 %collective-permute-start.6 = (f32[3,8,8,1]{3,2,1,0:T(8,128)S(1)}, f32[3,8,8,1]{3,2,1,0:T(8,128)S(1)}, u32[]{:S(2)}, u32[]{:S(2)}) collective-permute-start(f32[3,8,8,1]{3,2,1,0:T(8,128)S(1)} %get-tuple-element.198), channel_id=1, source_target_pairs={{0,16},{16,0},{1,17},{17,1},{2,18},{18,2},{3,19},{19,3},{4,20},{20... | collective-permute-start | bytes 2312 | tf_op jit(solution)/shard_map/ppermute | solution.py:19
  24.1 5.9 %collective-permute-start.7 = (f32[3,8,8,1]{3,2,1,0:T(8,128)S(1)}, f32[3,8,8,1]{3,2,1,0:T(8,128)S(1)}, u32[]{:S(2)}, u32[]{:S(2)}) collective-permute-start(f32[3,8,8,1]{3,2,1,0:T(8,128)S(1)} %get-tuple-element.199), channel_id=1, source_target_pairs={{16,0},{0,16},{17,1},{1,17},{18,2},{2,18},{19,3},{3,19},{20,4},{4,... | collective-permute-start | bytes 2312 | tf_op jit(solution)/shard_map/ppermute | solution.py:22
  33.6 6.1 %collective-permute-start.10 = (f32[3,10,1,130]{3,2,1,0:T(1,128)S(1)}, f32[3,10,1,130]{3,2,1,0:T(1,128)S(1)}, u32[]{:S(2)}, u32[]{:S(2)}) collective-permute-start(f32[3,10,1,130]{3,2,1,0:T(1,128)S(1)} %get-tuple-element.159), channel_id=1, source_target_pairs={{0,1},{1,2},{2,3},{3,0},{4,5},{5,6},{6,7},{7,4},{8,9},{9,10},{10,1... | collective-permute-start | bytes 46808 | tf_op jit(solution)/shard_map/ppermute | solution.py:19
  35.0 4.7 %collective-permute-start.11 = (f32[3,10,1,130]{3,2,1,0:T(1,128)S(1)}, f32[3,10,1,130]{3,2,1,0:T(1,128)S(1)}, u32[]{:S(2)}, u32[]{:S(2)}) collective-permute-start(f32[3,10,1,130]{3,2,1,0:T(1,128)S(1)} %get-tuple-element.160), channel_id=1, source_target_pairs={{1,0},{2,1},{3,2},{0,3},{5,4},{6,5},{7,6},{4,7},{9,8},{10,9},{11,1... | collective-permute-start | bytes 46808 | tf_op jit(solution)/shard_map/ppermute | solution.py:22
  40.3 5.7 %collective-permute-start.12 = (f32[3,8,8,1]{3,2,1,0:T(8,128)S(1)}, f32[3,8,8,1]{3,2,1,0:T(8,128)S(1)}, u32[]{:S(2)}, u32[]{:S(2)}) collective-permute-start(f32[3,8,8,1]{3,2,1,0:T(8,128)S(1)} %get-tuple-element.193), channel_id=1, source_target_pairs={{0,16},{16,0},{1,17},{17,1},{2,18},{18,2},{3,19},{19,3},{4,20},{20... | collective-permute-start | bytes 2312 | tf_op jit(solution)/shard_map/ppermute | solution.py:19
  41.7 5.5 %collective-permute-start.13 = (f32[3,8,8,1]{3,2,1,0:T(8,128)S(1)}, f32[3,8,8,1]{3,2,1,0:T(8,128)S(1)}, u32[]{:S(2)}, u32[]{:S(2)}) collective-permute-start(f32[3,8,8,1]{3,2,1,0:T(8,128)S(1)} %get-tuple-element.194), channel_id=1, source_target_pairs={{16,0},{0,16},{17,1},{1,17},{18,2},{2,18},{19,3},{3,19},{20,4},{4,... | collective-permute-start | bytes 2312 | tf_op jit(solution)/shard_map/ppermute | solution.py:22
  50.9 5.9 %collective-permute-start.16 = (f32[3,10,1,130]{3,2,1,0:T(1,128)S(1)}, f32[3,10,1,130]{3,2,1,0:T(1,128)S(1)}, u32[]{:S(2)}, u32[]{:S(2)}) collective-permute-start(f32[3,10,1,130]{3,2,1,0:T(1,128)S(1)} %get-tuple-element.157), channel_id=1, source_target_pairs={{0,1},{1,2},{2,3},{3,0},{4,5},{5,6},{6,7},{7,4},{8,9},{9,10},{10,1... | collective-permute-start | bytes 46808 | tf_op jit(solution)/shard_map/ppermute | solution.py:19
  52.1 4.7 %collective-permute-start.17 = (f32[3,10,1,130]{3,2,1,0:T(1,128)S(1)}, f32[3,10,1,130]{3,2,1,0:T(1,128)S(1)}, u32[]{:S(2)}, u32[]{:S(2)}) collective-permute-start(f32[3,10,1,130]{3,2,1,0:T(1,128)S(1)} %get-tuple-element.158), channel_id=1, source_target_pairs={{1,0},{2,1},{3,2},{0,3},{5,4},{6,5},{7,6},{4,7},{9,8},{10,9},{11,1... | collective-permute-start | bytes 46808 | tf_op jit(solution)/shard_map/ppermute | solution.py:22
  57.4 5.7 %collective-permute-start.18 = (f32[3,8,8,1]{3,2,1,0:T(8,128)S(1)}, f32[3,8,8,1]{3,2,1,0:T(8,128)S(1)}, u32[]{:S(2)}, u32[]{:S(2)}) collective-permute-start(f32[3,8,8,1]{3,2,1,0:T(8,128)S(1)} %get-tuple-element.188), channel_id=1, source_target_pairs={{0,16},{16,0},{1,17},{17,1},{2,18},{18,2},{3,19},{19,3},{4,20},{20... | collective-permute-start | bytes 2312 | tf_op jit(solution)/shard_map/ppermute | solution.py:19
  58.8 5.6 %collective-permute-start.19 = (f32[3,8,8,1]{3,2,1,0:T(8,128)S(1)}, f32[3,8,8,1]{3,2,1,0:T(8,128)S(1)}, u32[]{:S(2)}, u32[]{:S(2)}) collective-permute-start(f32[3,8,8,1]{3,2,1,0:T(8,128)S(1)} %get-tuple-element.189), channel_id=1, source_target_pairs={{16,0},{0,16},{17,1},{1,17},{18,2},{2,18},{19,3},{3,19},{20,4},{4,... | collective-permute-start | bytes 2312 | tf_op jit(solution)/shard_map/ppermute | solution.py:22
  68.0 6.0 %collective-permute-start.22 = (f32[3,10,1,130]{3,2,1,0:T(1,128)S(1)}, f32[3,10,1,130]{3,2,1,0:T(1,128)S(1)}, u32[]{:S(2)}, u32[]{:S(2)}) collective-permute-start(f32[3,10,1,130]{3,2,1,0:T(1,128)S(1)} %get-tuple-element.155), channel_id=1, source_target_pairs={{0,1},{1,2},{2,3},{3,0},{4,5},{5,6},{6,7},{7,4},{8,9},{9,10},{10,1... | collective-permute-start | bytes 46808 | tf_op jit(solution)/shard_map/ppermute | solution.py:19
  69.4 4.5 %collective-permute-start.23 = (f32[3,10,1,130]{3,2,1,0:T(1,128)S(1)}, f32[3,10,1,130]{3,2,1,0:T(1,128)S(1)}, u32[]{:S(2)}, u32[]{:S(2)}) collective-permute-start(f32[3,10,1,130]{3,2,1,0:T(1,128)S(1)} %get-tuple-element.156), channel_id=1, source_target_pairs={{1,0},{2,1},{3,2},{0,3},{5,4},{6,5},{7,6},{4,7},{9,8},{10,9},{11,1... | collective-permute-start | bytes 46808 | tf_op jit(solution)/shard_map/ppermute | solution.py:22
  74.5 5.7 %collective-permute-start.24 = (f32[3,8,8,1]{3,2,1,0:T(8,128)S(1)}, f32[3,8,8,1]{3,2,1,0:T(8,128)S(1)}, u32[]{:S(2)}, u32[]{:S(2)}) collective-permute-start(f32[3,8,8,1]{3,2,1,0:T(8,128)S(1)} %get-tuple-element.183), channel_id=1, source_target_pairs={{0,16},{16,0},{1,17},{17,1},{2,18},{18,2},{3,19},{19,3},{4,20},{20... | collective-permute-start | bytes 2312 | tf_op jit(solution)/shard_map/ppermute | solution.py:19
  75.9 5.7 %collective-permute-start.25 = (f32[3,8,8,1]{3,2,1,0:T(8,128)S(1)}, f32[3,8,8,1]{3,2,1,0:T(8,128)S(1)}, u32[]{:S(2)}, u32[]{:S(2)}) collective-permute-start(f32[3,8,8,1]{3,2,1,0:T(8,128)S(1)} %get-tuple-element.184), channel_id=1, source_target_pairs={{16,0},{0,16},{17,1},{1,17},{18,2},{2,18},{19,3},{3,19},{20,4},{4,... | collective-permute-start | bytes 2312 | tf_op jit(solution)/shard_map/ppermute | solution.py:22
  85.2 6.4 %collective-permute-start.28 = (f32[3,10,1,130]{3,2,1,0:T(1,128)S(1)}, f32[3,10,1,130]{3,2,1,0:T(1,128)S(1)}, u32[]{:S(2)}, u32[]{:S(2)}) collective-permute-start(f32[3,10,1,130]{3,2,1,0:T(1,128)S(1)} %get-tuple-element.153), channel_id=1, source_target_pairs={{0,1},{1,2},{2,3},{3,0},{4,5},{5,6},{6,7},{7,4},{8,9},{9,10},{10,1... | collective-permute-start | bytes 46808 | tf_op jit(solution)/shard_map/ppermute | solution.py:19
  86.7 4.9 %collective-permute-start.29 = (f32[3,10,1,130]{3,2,1,0:T(1,128)S(1)}, f32[3,10,1,130]{3,2,1,0:T(1,128)S(1)}, u32[]{:S(2)}, u32[]{:S(2)}) collective-permute-start(f32[3,10,1,130]{3,2,1,0:T(1,128)S(1)} %get-tuple-element.154), channel_id=1, source_target_pairs={{1,0},{2,1},{3,2},{0,3},{5,4},{6,5},{7,6},{4,7},{9,8},{10,9},{11,1... | collective-permute-start | bytes 46808 | tf_op jit(solution)/shard_map/ppermute | solution.py:22
  92.8 5.9 %collective-permute-start.30 = (f32[3,8,8,1]{3,2,1,0:T(8,128)}, f32[3,8,8,1]{3,2,1,0:T(8,128)S(1)}, u32[]{:S(2)}, u32[]{:S(2)}) collective-permute-start(f32[3,8,8,1]{3,2,1,0:T(8,128)} %get-tuple-element.178), channel_id=1, source_target_pairs={{0,16},{16,0},{1,17},{17,1},{2,18},{18,2},{3,19},{19,3},{4,20},{20... | collective-permute-start | bytes 2312 | tf_op jit(solution)/shard_map/ppermute | solution.py:19
  94.1 5.9 %collective-permute-start.31 = (f32[3,8,8,1]{3,2,1,0:T(8,128)}, f32[3,8,8,1]{3,2,1,0:T(8,128)S(1)}, u32[]{:S(2)}, u32[]{:S(2)}) collective-permute-start(f32[3,8,8,1]{3,2,1,0:T(8,128)} %get-tuple-element.179), channel_id=1, source_target_pairs={{16,0},{0,16},{17,1},{1,17},{18,2},{2,18},{19,3},{3,19},{20,4},{4,... | collective-permute-start | bytes 2312 | tf_op jit(solution)/shard_map/ppermute | solution.py:22
  103.6 6.1 %collective-permute-start.34 = (f32[3,10,1,130]{3,2,1,0:T(1,128)S(1)}, f32[3,10,1,130]{3,2,1,0:T(1,128)S(1)}, u32[]{:S(2)}, u32[]{:S(2)}) collective-permute-start(f32[3,10,1,130]{3,2,1,0:T(1,128)S(1)} %get-tuple-element.151), channel_id=1, source_target_pairs={{0,1},{1,2},{2,3},{3,0},{4,5},{5,6},{6,7},{7,4},{8,9},{9,10},{10,1... | collective-permute-start | bytes 46808 | tf_op jit(solution)/shard_map/ppermute | solution.py:19
  104.8 4.8 %collective-permute-start.35 = (f32[3,10,1,130]{3,2,1,0:T(1,128)S(1)}, f32[3,10,1,130]{3,2,1,0:T(1,128)S(1)}, u32[]{:S(2)}, u32[]{:S(2)}) collective-permute-start(f32[3,10,1,130]{3,2,1,0:T(1,128)S(1)} %get-tuple-element.152), channel_id=1, source_target_pairs={{1,0},{2,1},{3,2},{0,3},{5,4},{6,5},{7,6},{4,7},{9,8},{10,9},{11,1... | collective-permute-start | bytes 46808 | tf_op jit(solution)/shard_map/ppermute | solution.py:22
  (16 other events, 75.8 us)
where the time goes:
time: 161 us
  starting transfers between devices  48.3 us (30%)
  waiting for transfers between devices  47.8 us (30%)
  blocking collectives  40 us (25%)
  other arithmetic  7.89 us (5%)
  local copies, waits for them, and re-layouts  7.83 us (5%)
  matrix products  7.12 us (4%)
  between operations  2.05 us (1%)
    psum x1, blocking collectives, local(): lax.psum(jnp.dot(whole, newest[0], preferred_element_type=jnp.float32), (...  40 us
    ppermute x18, waiting for transfers between devices, padded_2(): lax.ppermute(lax.slice_in_dim(block, block.shape[dim] - width, None, axis...  39.4 us
    ppermute x18, starting transfers between devices, padded_2(): lax.ppermute(lax.slice_in_dim(block, 0, width, axis=dim), axis, backward)  29.4 us
    ppermute x18, starting transfers between devices, padded_2(): lax.ppermute(lax.slice_in_dim(block, block.shape[dim] - width, None, axis...  18.8 us
    ppermute x18, waiting for transfers between devices, padded_2(): lax.ppermute(lax.slice_in_dim(block, 0, width, axis=dim), axis, backward)  8.34 us
    slice x12, other arithmetic, padded_2(): lax.slice_in_dim(block, block.shape[dim] - width, None, axis=dim)  3.49 us
  transfers between devices with their start and end apart: 36, of which 25 were waited for; matrix products, arithmetic and copies ran while one was open for 2% of the time, Pallas kernels for 0%

commit v1 on v0

v1 whole, which is shorter than its diff:
```python
import functools

import jax
import jax.numpy as jnp
from jax import lax
from jax.experimental import pallas as pl
from jax.experimental.pallas import tpu as pltpu
from jax.sharding import PartitionSpec as P

NS_ITERS = 8
STAGES = 6
MESH = pl.DeviceIdType.MESH

time_step = 0.1
viscosity = 0.05


def each(count, body):
    if count <= 8:
        for i in range(count):
            body(i)
    else:
        lax.fori_loop(0, count, lambda i, carry: (body(i), carry)[1], 0)


def kernel(
    sizes, rows_total, v_ref, earlier_ref,
    field_ref, level_ref, basis_ref,
    stage, zsend, xsend, yrecv, zrecv, xrecv,
    gram_ref, part_ref, plane_ref, line_ref, full_ref,
    cross_send, cross_plane, cross_mid, cross_line,
    ysend_sem, yrecv_sem, zsend_sem, zrecv_sem, xsend_sem, xrecv_sem,
    asend_sem, arecv_sem, bsend_sem, brecv_sem, csend_sem, crecv_sem,
    dsend_sem, drecv_sem, esend_sem, erecv_sem,
):
    n_grp, n_gy, n_gz = sizes
    grp, gy, gz = lax.axis_index("grp"), lax.axis_index("gy"), lax.axis_index("gz")
    n_plane = n_grp * n_gy
    me = grp * n_gy + gy
    comps, ny, nz, nx = v_ref.shape
    ranks = earlier_ref.shape[0]
    lines = comps * ny

    def plane_id(offset):
        peer = lax.rem(me + offset, n_plane)
        return peer, {"grp": peer // n_gy, "gy": lax.rem(peer, n_gy)}

    def line_id(offset):
        peer = lax.rem(gz + offset, n_gz)
        return peer, {"gz": peer}

    y_up, y_down = {"gy": lax.rem(gy + 1, n_gy)}, {"gy": lax.rem(gy + n_gy - 1, n_gy)}
    z_up, z_down = {"gz": lax.rem(gz + 1, n_gz)}, {"gz": lax.rem(gz + n_gz - 1, n_gz)}
    x_up, x_down = {"grp": lax.rem(grp + 1, n_grp)}, {"grp": lax.rem(grp + n_grp - 1, n_grp)}
    x_ways = 1 if n_grp == 2 else 2

    barrier = pltpu.get_barrier_semaphore()

    def greet_plane(i):
        pl.semaphore_signal(barrier, inc=1, device_id=plane_id(i + 1)[1], device_id_type=MESH)

    def greet_line(i):
        pl.semaphore_signal(barrier, inc=1, device_id=line_id(i + 1)[1], device_id_type=MESH)

    each(n_plane - 1, greet_plane)
    each(n_gz - 1, greet_line)
    pl.semaphore_wait(barrier, n_plane + n_gz - 2)

    def remote(src, dst, send_sem, recv_sem, target):
        return pltpu.make_async_remote_copy(
            src_ref=src, dst_ref=dst, send_sem=send_sem, recv_sem=recv_sem,
            device_id=target, device_id_type=MESH,
        )

    def halo_copies(s):
        copies = [
            remote(stage.at[s, :, ny - 1], yrecv.at[s, 0], ysend_sem.at[s, 0], yrecv_sem.at[s, 0], y_up),
            remote(stage.at[s, :, 0], yrecv.at[s, 1], ysend_sem.at[s, 1], yrecv_sem.at[s, 1], y_down),
            remote(zsend.at[s, 0], zrecv.at[s, 0], zsend_sem.at[s, 0], zrecv_sem.at[s, 0], z_up),
            remote(zsend.at[s, 1], zrecv.at[s, 1], zsend_sem.at[s, 1], zrecv_sem.at[s, 1], z_down),
            remote(xsend.at[s], xrecv.at[s, 0], xsend_sem.at[s, 0], xrecv_sem.at[s, 0], x_up),
        ]
        if x_ways == 2:
            copies.append(
                remote(xsend.at[s], xrecv.at[s, 1], xsend_sem.at[s, 1], xrecv_sem.at[s, 1], x_down)
            )
        return copies

    lane = lax.broadcasted_iota(jnp.int32, (lines, nz, nx), 2)
    line = lax.broadcasted_iota(jnp.int32, (lines, nz, nx), 0)
    row = lax.broadcasted_iota(jnp.int32, (lines, nz, nx), 1)
    low_lane = lane == line
    high_lane = lane == line + nx // 2

    def send(s, f):
        stage[s] = f
        zsend[s, 0] = f[:, :, nz - 1, :]
        zsend[s, 1] = f[:, :, 0, :]
        flat = f.reshape(lines, nz, nx)
        packed = jnp.where(low_lane, flat[:, :, 0:1], 0.0)
        packed = packed + jnp.where(high_lane, flat[:, :, nx - 1 : nx], 0.0)
        xsend[s] = jnp.sum(packed, axis=0)
        copies = halo_copies(s)
        for copy in copies:
            copy.start()
        return copies

    def stepped(s, f, copies):
        for copy in copies:
            copy.wait_recv()
        flat = f.reshape(lines, nz, nx)
        bottom = jnp.where(gy == 0, 0.0, yrecv[s, 0])
        upper = jnp.where(gy == n_gy - 1, 0.0, yrecv[s, 1])
        y_minus = jnp.concatenate([bottom[:, None], f[:, :-1]], axis=1)
        y_plus = jnp.concatenate([f[:, 1:], upper[:, None]], axis=1)
        z_low = zrecv[s, 0].reshape(lines, 1, nx)
        z_high = zrecv[s, 1].reshape(lines, 1, nx)
        z_minus = jnp.where(row == 0, z_low, pltpu.roll(flat, 1, 1)).reshape(f.shape)
        z_plus = jnp.where(row == nz - 1, z_high, pltpu.roll(flat, nz - 1, 1)).reshape(f.shape)
        from_left, from_right = xrecv[s, 0], xrecv[s, x_ways - 1]
        x_low = jnp.sum(jnp.where(high_lane, from_left[None], 0.0), axis=2, keepdims=True)
        x_high = jnp.sum(jnp.where(low_lane, from_right[None], 0.0), axis=2, keepdims=True)
        x_minus = jnp.where(lane == 0, x_low, pltpu.roll(flat, 1, 2)).reshape(f.shape)
        x_plus = jnp.where(lane == nx - 1, x_high, pltpu.roll(flat, nx - 1, 2)).reshape(f.shape)
        carried = f[0][None] * (x_plus - x_minus) * 0.5
        carried = carried + f[1][None] * (y_plus - y_minus) * 0.5
        carried = carried + f[2][None] * (z_plus - z_minus) * 0.5
        spread = x_plus + x_minus + y_plus + y_minus + z_plus + z_minus - 6.0 * f
        return f + time_step * (viscosity * spread - carried)

    def scatter_copy(i):
        peer, target = plane_id(i + 1)
        return remote(
            gram_ref.at[peer], plane_ref.at[me], asend_sem.at[i], arecv_sem.at[me], target
        )

    def line_copy(i):
        _, target = line_id(i + 1)
        return remote(part_ref, line_ref.at[gz], bsend_sem.at[i], brecv_sem.at[gz], target)

    def gather_copy(i):
        _, target = plane_id(i + 1)
        return remote(
            full_ref.at[me], full_ref.at[me], csend_sem.at[i], crecv_sem.at[me], target
        )

    def cross_plane_copy(i):
        _, target = plane_id(i + 1)
        return remote(cross_send, cross_plane.at[me], dsend_sem.at[i], drecv_sem.at[me], target)

    def cross_line_copy(i):
        _, target = line_id(i + 1)
        return remote(cross_mid, cross_line.at[gz], esend_sem.at[i], erecv_sem.at[gz], target)

    def wait_plane(buffer, sem):
        def body(i):
            peer, target = plane_id(i + 1)
            remote(buffer.at[peer], buffer.at[peer], sem.at[peer], sem.at[peer], target).wait_recv()

        each(n_plane - 1, body)

    def wait_line(buffer, sem):
        def body(i):
            peer, target = line_id(i + 1)
            remote(buffer.at[peer], buffer.at[peer], sem.at[peer], sem.at[peer], target).wait_recv()

        each(n_gz - 1, body)

    def begin_gram():
        earlier = earlier_ref[...]
        gram = lax.dot_general(
            earlier, earlier, (((1,), (1,)), ((), ())), preferred_element_type=jnp.float32
        )
        gram_ref[...] = gram.reshape(gram_ref.shape)
        plane_ref[me] = gram_ref[me]
        each(n_plane - 1, lambda i: scatter_copy(i).start())

    def add_plane():
        wait_plane(plane_ref, arecv_sem)
        part = jnp.sum(plane_ref[...], axis=0)
        part_ref[...] = part
        line_ref[gz] = part
        each(n_gz - 1, lambda i: line_copy(i).start())

    def add_line():
        wait_line(line_ref, brecv_sem)
        full_ref[me] = jnp.sum(line_ref[...], axis=0)
        each(n_plane - 1, lambda i: gather_copy(i).start())

    between = {0: begin_gram, 2: add_plane, 3: add_line}
    base = v_ref[...]
    f = base
    for s in range(STAGES):
        copies = send(s, f)
        if s in between:
            between[s]()
        moved = stepped(s, f, copies)
        if s % 3 == 0:
            f = moved
        elif s % 3 == 1:
            f = 0.75 * base + 0.25 * moved
        else:
            f = base / 3.0 + 2.0 / 3.0 * moved
            base = f
    field_ref[...] = f

    blocks = [(c, y, z) for c in range(comps) for y in range(0, ny, 2) for z in range(0, nz, 2)]

    def newest_block(b):
        c, y, z = blocks[b]
        return field_ref[c, y, pl.ds(z, 1), :].astype(jnp.bfloat16).astype(jnp.float32)

    total = jnp.zeros((ranks, nx), jnp.float32)
    own = jnp.zeros((1, nx), jnp.float32)
    for b in range(len(blocks)):
        newest = newest_block(b)
        total = total + earlier_ref[:, b * nx : (b + 1) * nx].astype(jnp.float32) * newest
        own = own + newest * newest
    square_row = lax.broadcasted_iota(jnp.int32, (ranks, ranks), 0)
    square_col = lax.broadcasted_iota(jnp.int32, (ranks, ranks), 1)
    total = jnp.where(lax.broadcasted_iota(jnp.int32, (ranks, nx), 0) == ranks - 1, own, total)
    cross = jnp.sum(total.T, axis=0, keepdims=True)
    cross_send[...] = jnp.broadcast_to(cross, cross_send.shape)
    cross_plane[me] = cross_send[...]
    each(n_plane - 1, lambda i: cross_plane_copy(i).start())
    wait_plane(full_ref, crecv_sem)
    wait_plane(cross_plane, drecv_sem)
    cross_mid[...] = jnp.sum(cross_plane[...], axis=0)
    cross_line[gz] = cross_mid[...]
    each(n_gz - 1, lambda i: cross_line_copy(i).start())
    wait_line(cross_line, erecv_sem)
    cross = jnp.sum(cross_line[...], axis=0)[0:1]
    cross = jnp.broadcast_to(cross, (ranks, ranks))

    gram = full_ref[...].reshape(ranks, ranks)
    gram = jnp.where(square_col == ranks - 1, cross.T, gram)
    gram = jnp.where(square_row == ranks - 1, cross, gram)
    scale = jnp.sqrt(jnp.sum(gram * gram, keepdims=True))
    level = gram / scale
    ident = jnp.where(square_row == square_col, 1.0, 0.0)
    dot = functools.partial(
        jnp.dot, precision=lax.Precision.HIGHEST, preferred_element_type=jnp.float32
    )
    inverse = ident
    for repeat in range(NS_ITERS):
        product = level if repeat == 0 else dot(inverse, level)
        factor = 1.5 * ident - 0.5 * product
        level = dot(level, factor)
        inverse = factor if repeat == 0 else dot(factor, inverse)
    level_ref[...] = level
    factor = jnp.sqrt(jnp.full((1, 1), rows_total, jnp.float32)) / jnp.sqrt(scale)
    weights = (inverse * factor).astype(jnp.bfloat16)
    last = lax.broadcasted_iota(jnp.int32, (ranks, nx), 0) == ranks - 1
    for b in range(len(blocks)):
        block = earlier_ref[:, b * nx : (b + 1) * nx].astype(jnp.float32)
        block = jnp.where(last, newest_block(b), block).astype(jnp.bfloat16)
        basis_ref[:, b * nx : (b + 1) * nx] = jnp.dot(
            weights, block, preferred_element_type=jnp.float32
        ).astype(jnp.bfloat16)

    for s in range(STAGES):
        for copy in halo_copies(s):
            copy.wait_send()
    each(n_plane - 1, lambda i: scatter_copy(i).wait_send())
    each(n_gz - 1, lambda i: line_copy(i).wait_send())
    each(n_plane - 1, lambda i: gather_copy(i).wait_send())
    each(n_plane - 1, lambda i: cross_plane_copy(i).wait_send())
    each(n_gz - 1, lambda i: cross_line_copy(i).wait_send())


def local(velocity, basis_old, strength, snapshots):
    modes = basis_old.shape[0]
    earlier_count = snapshots.shape[0]
    ranks = modes + earlier_count + 1
    sizes = tuple(lax.axis_size(axis) for axis in ("grp", "gy", "gz"))
    n_grp, n_gy, n_gz = sizes
    n_plane = n_grp * n_gy
    comps, ny, nz, nx = velocity.shape
    head = (strength[:, None] * basis_old.reshape(modes, -1).astype(jnp.float32)).astype(
        jnp.bfloat16
    )
    length = head.shape[1]
    earlier = jnp.concatenate(
        [head, snapshots.reshape(earlier_count, -1), jnp.zeros((1, length), jnp.bfloat16)], axis=0
    )
    share = ranks // n_plane
    assert share * n_plane == ranks
    f32 = jnp.float32
    dma = pltpu.SemaphoreType.DMA
    vmem = pl.BlockSpec(memory_space=pltpu.VMEM)
    field, level, basis_new = pl.pallas_call(
        functools.partial(kernel, sizes, float(length * n_plane * n_gz)),
        out_shape=(
            jax.ShapeDtypeStruct(velocity.shape, f32),
            jax.ShapeDtypeStruct((ranks, ranks), f32),
            jax.ShapeDtypeStruct((ranks, length), jnp.bfloat16),
        ),
        in_specs=[vmem, vmem],
        out_specs=(vmem, vmem, vmem),
        scratch_shapes=[
            pltpu.VMEM((STAGES,) + velocity.shape, f32),
            pltpu.VMEM((STAGES, 2, comps, ny, nx), f32),
            pltpu.VMEM((STAGES, nz, nx), f32),
            pltpu.VMEM((STAGES, 2, comps, nz, nx), f32),
            pltpu.VMEM((STAGES, 2, comps, ny, nx), f32),
            pltpu.VMEM((STAGES, 2, nz, nx), f32),
            pltpu.VMEM((n_plane, share, ranks), f32),
            pltpu.VMEM((share, ranks), f32),
            pltpu.VMEM((n_plane, share, ranks), f32),
            pltpu.VMEM((n_gz, share, ranks), f32),
            pltpu.VMEM((n_plane, share, ranks), f32),
            pltpu.VMEM((8, ranks), f32),
            pltpu.VMEM((n_plane, 8, ranks), f32),
            pltpu.VMEM((8, ranks), f32),
            pltpu.VMEM((n_gz, 8, ranks), f32),
            dma((STAGES, 2)), dma((STAGES, 2)),
            dma((STAGES, 2)), dma((STAGES, 2)),
            dma((STAGES, 2)), dma((STAGES, 2)),
            dma((n_plane,)), dma((n_plane,)),
            dma((n_gz,)), dma((n_gz,)),
            dma((n_plane,)), dma((n_plane,)),
            dma((n_plane,)), dma((n_plane,)),
            dma((n_gz,)), dma((n_gz,)),
        ],
        compiler_params=pltpu.CompilerParams(
            collective_id=0, has_side_effects=True, vmem_limit_bytes=24 * 1024 * 1024
        ),
    )(velocity, earlier)
    basis_new = basis_new.reshape(ranks, comps, ny // 2, nz // 2, nx)
    return (field, basis_new, level)


def solution(mesh):
    placed = (
        P(None, "gy", "gz", "grp"),
        P(None, None, "gy", "gz", "grp"),
        P(),
        P(None, None, "gy", "gz", "grp"),
    )
    return jax.shard_map(
        local,
        mesh=mesh,
        in_specs=placed,
        out_specs=(P(None, "gy", "gz", "grp"), P(None, None, "gy", "gz", "grp"), P()),
        check_vma=False,
    )
```

time: 161 us -> 49.2 us (0.31)
  starting transfers between devices: 48.3 us -> 0 us
  waiting for transfers between devices: 47.8 us -> 0 us
  Pallas kernels: 0 us -> 41.7 us
  blocking collectives: 40 us -> 0 us
  other arithmetic: 7.89 us -> 0.52 us
  matrix products: 7.12 us -> 0 us
  local copies, waits for them, and re-layouts: 7.83 us -> 6.09 us
    ppermute x36 -> x0, starting transfers between devices: 48.3 us -> none  [the longest x18 29.4 us: padded_2(): lax.ppermute(lax.slice_in_dim(block, 0, width, axis=dim), axis, backward)]
    ppermute x36 -> x0, waiting for transfers between devices: 47.8 us -> none  [the longest x18 39.4 us: padded_2(): lax.ppermute(lax.slice_in_dim(block, block.shape[dim] - width, None, axis...]
    pallas_call x0 -> x1, Pallas kernels: none -> 41.7 us  [local(): pl.pallas_call(functools.partial(kernel, sizes, float(length * n_plane *...]
    psum x1 -> x0, blocking collectives: 40 us -> none  [local(): lax.psum(jnp.dot(whole, newest[0], preferred_element_type=jnp.float32), (...]
    dot_general x27 -> x0, matrix products: 7.12 us -> none  [the longest x8 2.26 us: local(): level = jnp.dot(level, factor, precision=lax.Precision.HIGHEST)]
    slice x12 -> x0, other arithmetic: 3.49 us -> none  [padded_2(): lax.slice_in_dim(block, block.shape[dim] - width, None, axis=dim)]
    slice x7 -> x0, local copies, waits for them, and re-layouts: 2.44 us -> none  [the longest x6 2.13 us: padded_2(): lax.slice_in_dim(block, block.shape[dim] - width, None, axis=dim)]
    concatenate x6 -> x1, other arithmetic: 2.22 us -> 0.36 us  [local(): jnp.concatenate([head, snapshots.reshape(earlier_count, -1), jnp.zeros((1...]
  transfers between devices with their start and end apart: 36 -> 0, of which waited for: 25 -> 0; matrix products, arithmetic and copies ran while one was open for 2% -> 0% of each run, Pallas kernels for 0% -> 0%
where the time goes in v1:
time: 49.2 us; the launch traced here: 49 us
  Pallas kernels  41.7 us (85%)
  local copies, waits for them, and re-layouts  6.09 us (12%)
  between operations  0.7 us (1%)
  other arithmetic  0.52 us (1%)
    pallas_call x1, Pallas kernels, local(): pl.pallas_call(functools.partial(kernel, sizes, float(length * n_plane *...  41.7 us
    reshape x1, local copies, waits for them, and re-layouts, local(): basis_new = basis_new.reshape(ranks, comps, ny // 2, nz // 2, nx)  2.02 us
    unnamed x8, local copies, waits for them, and re-layouts  1.8 us
    reshape x1, local copies, waits for them, and re-layouts, local(): snapshots.reshape(earlier_count, -1)  1.79 us

profile of v1, /device:TPU:0, one launch (start us, length us, event | category | flops | bytes accessed | tf_op | source)
XLA Modules:
  0.0 49.0 jit_solution(12524507345327960738)
XLA Ops:
  0.6 0.0 copy-start.1
  0.6 0.1 pad.2.clone
  0.7 0.0 copy-start.2
  0.7 1.8 %reshape.16 = bf16[63,6144]{1,0:T(8,128)(2,1)S(1)} reshape(bf16[63,3,4,4,128]{4,3,2,1,0:T(4,128)(2,1)} %param.7) | data formatting | bytes 1548288 | tf_op jit(solution)/shard_map/reshape | solution.py:284
  2.5 0.0 copy-done.1
  2.5 0.4 reshape.18
  2.9 0.0 copy-done.2
  2.9 0.2 multiply_convert_fusion
  3.1 0.0 copy-start
  3.1 0.4 maximum_maximum_fusion.earlier_ref
  3.5 0.5 %copy-done = f32[3,8,8,128]{3,2,1,0:T(8,128)S(1)} copy-done((f32[3,8,8,128]{3,2,1,0:T(8,128)S(1)}, f32[3,8,8,128]{3,2,1,0:T(8,128)}, u32[]{:S(2)}) %copy-start) | copy-done | bytes 98328
  4.0 41.7 %shard_map.67 = (f32[3,8,8,128]{3,2,1,0:T(8,128)S(1)}, f32[128,128]{1,0:T(8,128)S(1)}, bf16[128,6144]{1,0:T(8,128)(2,1)S(1)}) custom-call(f32[3,8,8,128]{3,2,1,0:T(8,128)S(1)} %copy-done, bf16[128,6144]{1,0:T(8,128)(2,1)S(1)} %maximum_maximum_fusion.earlier_ref), custom_call_target="tpu_custom_call" | custom-call | tf_op jit(solution)/shard_map/pallas_call | solution.py:291
  45.7 2.0 %reshape.17 = bf16[128,3,4,4,128]{4,3,2,1,0:T(4,128)(2,1)} reshape(bf16[128,6144]{1,0:T(8,128)(2,1)S(1)} %get-tuple-element.7) | data formatting | bytes 3145728 | tf_op jit(solution)/shard_map/reshape | solution.py:329
  47.8 0.6 %copy.9 = f32[3,8,8,128]{3,2,1,0:T(8,128)} copy(f32[3,8,8,128]{3,2,1,0:T(8,128)S(1)} %get-tuple-element.12) | data formatting | bytes 196608
  48.4 0.6 %copy.10 = f32[128,128]{1,0:T(8,128)} copy(f32[128,128]{1,0:T(8,128)S(1)} %get-tuple-element.14) | data formatting | bytes 131072
Async XLA Ops:
  0.6 1.9 %copy-start.1 = (bf16[64,3,4,4,128]{4,3,2,1,0:T(4,128)(2,1)S(1)}, bf16[64,3,4,4,128]{4,3,2,1,0:T(4,128)(2,1)}, u32[]{:S(2)}) copy-start(bf16[64,3,4,4,128]{4,3,2,1,0:T(4,128)(2,1)} %param.5) | copy-start | bytes 2359300
  0.7 2.2 %copy-start.2 = (f32[64]{0:T(128)S(1)}, f32[64]{0:T(128)}, u32[]{:S(2)}) copy-start(f32[64]{0:T(128)} %param.6) | copy-start | bytes 772
  3.1 0.9 %copy-start = (f32[3,8,8,128]{3,2,1,0:T(8,128)S(1)}, f32[3,8,8,128]{3,2,1,0:T(8,128)}, u32[]{:S(2)}) copy-start(f32[3,8,8,128]{3,2,1,0:T(8,128)} %v_ref.1) | copy-start | bytes 294916

commit v2 on v1

--- a/solution.py
+++ b/solution.py
@@ -24,8 +24,9 @@
 
 
 def kernel(
-    sizes, rows_total, v_ref, earlier_ref,
-    field_ref, level_ref, basis_ref,
+    sizes, rows_total, v_ref, strength_ref, old_hbm, snap_hbm,
+    field_ref, level_ref, weights_ref, earlier_ref,
+    old_ref, snap_ref, wide_ref, load_sem,
     stage, zsend, xsend, yrecv, zrecv, xrecv,
     gram_ref, part_ref, plane_ref, line_ref, full_ref,
     cross_send, cross_plane, cross_mid, cross_line,
@@ -54,6 +55,12 @@
     x_up, x_down = {"grp": lax.rem(grp + 1, n_grp)}, {"grp": lax.rem(grp + n_grp - 1, n_grp)}
     x_ways = 1 if n_grp == 2 else 2
 
+    loads = [
+        pltpu.make_async_copy(old_hbm, old_ref, load_sem.at[0]),
+        pltpu.make_async_copy(snap_hbm, snap_ref, load_sem.at[1]),
+    ]
+    for load in loads:
+        load.start()
     barrier = pltpu.get_barrier_semaphore()
 
     def greet_plane(i):
@@ -166,7 +173,29 @@
 
         each(n_gz - 1, body)
 
+    modes, count = old_ref.shape[0], old_ref.shape[1]
+
+    def flatten():
+        for load in loads:
+            load.wait()
+
+        def scale_row(r, carry):
+            wide_ref[pl.ds(r * count, count), :] = strength_ref[r] * old_ref[r].astype(jnp.float32)
+            return carry
+
+        def copy_row(r, carry):
+            wide_ref[pl.ds((r + modes) * count, count), :] = snap_ref[r].astype(jnp.float32)
+            return carry
+
+        lax.fori_loop(0, modes, scale_row, 0, unroll=8)
+        lax.fori_loop(0, snap_ref.shape[0], copy_row, 0, unroll=7)
+        wide_ref[pl.ds((ranks - 1) * count, count), :] = jnp.zeros((count, nx), jnp.float32)
+        for b in range(count):
+            column = wide_ref[pl.ds(b, ranks, stride=count), :]
+            earlier_ref[:, b * nx : (b + 1) * nx] = column.astype(jnp.bfloat16)
+
     def begin_gram():
+        flatten()
         earlier = earlier_ref[...]
         gram = lax.dot_general(
             earlier, earlier, (((1,), (1,)), ((), ())), preferred_element_type=jnp.float32
@@ -223,6 +252,12 @@
     cross_send[...] = jnp.broadcast_to(cross, cross_send.shape)
     cross_plane[me] = cross_send[...]
     each(n_plane - 1, lambda i: cross_plane_copy(i).start())
+    tail = slice(ranks - 16, ranks)
+    last = lax.broadcasted_iota(jnp.int32, (16, nx), 0) == 15
+    for b in range(len(blocks)):
+        columns = slice(b * nx, (b + 1) * nx)
+        rows = earlier_ref[tail, columns].astype(jnp.float32)
+        earlier_ref[tail, columns] = jnp.where(last, newest_block(b), rows).astype(jnp.bfloat16)
     wait_plane(full_ref, crecv_sem)
     wait_plane(cross_plane, drecv_sem)
     cross_mid[...] = jnp.sum(cross_plane[...], axis=0)
@@ -250,13 +285,7 @@
     level_ref[...] = level
     factor = jnp.sqrt(jnp.full((1, 1), rows_total, jnp.float32)) / jnp.sqrt(scale)
     weights = (inverse * factor).astype(jnp.bfloat16)
-    last = lax.broadcasted_iota(jnp.int32, (ranks, nx), 0) == ranks - 1
-    for b in range(len(blocks)):
-        block = earlier_ref[:, b * nx : (b + 1) * nx].astype(jnp.float32)
-        block = jnp.where(last, newest_block(b), block).astype(jnp.bfloat16)
-        basis_ref[:, b * nx : (b + 1) * nx] = jnp.dot(
-            weights, block, preferred_element_type=jnp.float32
-        ).astype(jnp.bfloat16)
+    weights_ref[...] = weights
 
     for s in range(STAGES):
         for copy in halo_copies(s):
@@ -268,6 +297,23 @@
     each(n_gz - 1, lambda i: cross_line_copy(i).wait_send())
 
 
+def rotate(field_in, level_in, weights_ref, whole_ref, field_ref, level_ref, basis_ref, wide_ref):
+    field_ref[...] = field_in[...]
+    level_ref[...] = level_in[...]
+    ranks, count, nx = basis_ref.shape
+    weights = weights_ref[...]
+    for b in range(count):
+        wide_ref[pl.ds(b, ranks, stride=count), :] = jnp.dot(
+            weights, whole_ref[:, b * nx : (b + 1) * nx], preferred_element_type=jnp.float32
+        )
+
+    def write(r, carry):
+        basis_ref[r] = wide_ref[pl.ds(r * count, count), :].astype(jnp.bfloat16)
+        return carry
+
+    lax.fori_loop(0, ranks, write, 0, unroll=8)
+
+
 def local(velocity, basis_old, strength, snapshots):
     modes = basis_old.shape[0]
     earlier_count = snapshots.shape[0]
@@ -276,28 +322,33 @@
     n_grp, n_gy, n_gz = sizes
     n_plane = n_grp * n_gy
     comps, ny, nz, nx = velocity.shape
-    head = (strength[:, None] * basis_old.reshape(modes, -1).astype(jnp.float32)).astype(
-        jnp.bfloat16
-    )
-    length = head.shape[1]
-    earlier = jnp.concatenate(
-        [head, snapshots.reshape(earlier_count, -1), jnp.zeros((1, length), jnp.bfloat16)], axis=0
-    )
+    count = comps * (ny // 2) * (nz // 2)
+    length = count * nx
     share = ranks // n_plane
     assert share * n_plane == ranks
     f32 = jnp.float32
     dma = pltpu.SemaphoreType.DMA
     vmem = pl.BlockSpec(memory_space=pltpu.VMEM)
-    field, level, basis_new = pl.pallas_call(
+    field, level, weights, whole = pl.pallas_call(
         functools.partial(kernel, sizes, float(length * n_plane * n_gz)),
         out_shape=(
             jax.ShapeDtypeStruct(velocity.shape, f32),
             jax.ShapeDtypeStruct((ranks, ranks), f32),
+            jax.ShapeDtypeStruct((ranks, ranks), jnp.bfloat16),
             jax.ShapeDtypeStruct((ranks, length), jnp.bfloat16),
         ),
-        in_specs=[vmem, vmem],
-        out_specs=(vmem, vmem, vmem),
+        in_specs=[
+            vmem,
+            pl.BlockSpec(memory_space=pltpu.SMEM),
+            pl.BlockSpec(memory_space=pltpu.HBM),
+            pl.BlockSpec(memory_space=pltpu.HBM),
+        ],
+        out_specs=(vmem, vmem, vmem, vmem),
         scratch_shapes=[
+            pltpu.VMEM((modes, count, nx), jnp.bfloat16),
+            pltpu.VMEM((earlier_count, count, nx), jnp.bfloat16),
+            pltpu.VMEM((ranks * count, nx), f32),
+            dma((2,)),
             pltpu.VMEM((STAGES,) + velocity.shape, f32),
             pltpu.VMEM((STAGES, 2, comps, ny, nx), f32),
             pltpu.VMEM((STAGES, nz, nx), f32),
@@ -325,7 +376,19 @@
         compiler_params=pltpu.CompilerParams(
             collective_id=0, has_side_effects=True, vmem_limit_bytes=24 * 1024 * 1024
         ),
-    )(velocity, earlier)
+    )(velocity, strength, basis_old.reshape(modes, count, nx), snapshots.reshape(earlier_count, count, nx))
+    field, level, basis_new = pl.pallas_call(
+        rotate,
+        out_shape=(
+            jax.ShapeDtypeStruct(velocity.shape, f32),
+            jax.ShapeDtypeStruct((ranks, ranks), f32),
+            jax.ShapeDtypeStruct((ranks, count, nx), jnp.bfloat16),
+        ),
+        in_specs=[vmem, vmem, vmem, vmem],
+        out_specs=(vmem, vmem, vmem),
+        scratch_shapes=[pltpu.VMEM((ranks * count, nx), f32)],
+        compiler_params=pltpu.CompilerParams(vmem_limit_bytes=16 * 1024 * 1024),
+    )(field, level, weights, whole)
     basis_new = basis_new.reshape(ranks, comps, ny // 2, nz // 2, nx)
     return (field, basis_new, level)
 

time: 49.2 us -> 49.5 us (level)
  Pallas kernels: 41.7 us -> 44.8 us
  local copies, waits for them, and re-layouts: 6.09 us -> 3.8 us
  other arithmetic: 0.52 us -> 0 us
    reshape x2 -> x0, local copies, waits for them, and re-layouts: 3.81 us -> none  [the longest x1 2.02 us: local(): basis_new = basis_new.reshape(ranks, comps, ny // 2, nz // 2, nx)]
    pallas_call x0 -> x1, Pallas kernels: none -> 2.78 us  [local(): pl.pallas_call(rotate, out_shape=(jax.ShapeDtypeStruct(velocity.shape, f3...]
    unnamed x8, local copies, waits for them, and re-layouts: 1.8 us -> 3.8 us
where the time goes in v2:
time: 49.5 us; the launch traced here: 49.3 us
  Pallas kernels  44.8 us (91%)
  local copies, waits for them, and re-layouts  3.8 us (8%)
  between operations  0.65 us (1%)
    pallas_call x1, Pallas kernels, local(): pl.pallas_call(functools.partial(kernel, sizes, float(length * n_plane *...  42 us
    unnamed x8, local copies, waits for them, and re-layouts  3.8 us
    pallas_call x1, Pallas kernels, local(): pl.pallas_call(rotate, out_shape=(jax.ShapeDtypeStruct(velocity.shape, f3...  2.78 us

profile of v2, /device:TPU:0, one launch (start us, length us, event | category | flops | bytes accessed | tf_op | source)
XLA Modules:
  0.0 49.3 jit_solution(18260445052542327653)
XLA Ops:
  0.6 0.0 copy-start
  0.6 1.1 %copy-done = bf16[64,3,4,4,128]{4,3,2,1,0:T(4,128)(2,1)S(1)} copy-done((bf16[64,3,4,4,128]{4,3,2,1,0:T(4,128)(2,1)S(1)}, bf16[64,3,4,4,128]{4,3,2,1,0:T(4,128)(2,1)}, u32[]{:S(2)}) %copy-start) | copy-done | bytes 786456
  1.8 0.0 copy-start.1
  1.8 1.1 %copy-done.1 = bf16[63,3,4,4,128]{4,3,2,1,0:T(4,128)(2,1)S(1)} copy-done((bf16[63,3,4,4,128]{4,3,2,1,0:T(4,128)(2,1)S(1)}, bf16[63,3,4,4,128]{4,3,2,1,0:T(4,128)(2,1)}, u32[]{:S(2)}) %copy-start.1) | copy-done | bytes 774168
  2.9 0.0 copy-start.2
  2.9 0.9 %copy-done.2 = f32[3,8,8,128]{3,2,1,0:T(8,128)S(1)} copy-done((f32[3,8,8,128]{3,2,1,0:T(8,128)S(1)}, f32[3,8,8,128]{3,2,1,0:T(8,128)}, u32[]{:S(2)}) %copy-start.2) | copy-done | bytes 98328
  3.8 0.0 copy-start.3
  3.8 0.7 %copy-done.3 = f32[64]{0:T(128)S(1)} copy-done((f32[64]{0:T(128)S(1)}, f32[64]{0:T(128)}, u32[]{:S(2)}) %copy-start.3) | copy-done | bytes 280
  4.4 42.0 %shard_map.67 = (f32[3,8,8,128]{3,2,1,0:T(8,128)S(1)}, f32[128,128]{1,0:T(8,128)S(1)}, bf16[128,128]{1,0:T(8,128)(2,1)S(1)}, bf16[128,6144]{1,0:T(8,128)(2,1)S(1)}) custom-call(f32[3,8,8,128]{3,2,1,0:T(8,128)S(1)} %copy-done.2, f32[64]{0:T(128)S(1)} %copy-done.3, bf16[64,48,128]{2,1,0:T(8,128)(2,1)S(1)} %bitcast.3, bf16[63,48,128]{2,1,0:T(8,128)(2,1)S(1)} %bitcast.4), custom_call_target="tpu_custom_call" | custom-call | tf_op jit(solution)/shard_map/pallas_call | solution.py:332
  46.5 2.8 %shard_map.68 = (f32[3,8,8,128]{3,2,1,0:T(8,128)}, f32[128,128]{1,0:T(8,128)}, bf16[128,48,128]{2,1,0:T(8,128)(2,1)}) custom-call(f32[3,8,8,128]{3,2,1,0:T(8,128)S(1)} %get-tuple-element.10.field_in, f32[128,128]{1,0:T(8,128)S(1)} %get-tuple-element.11.level_in, bf16[128,128]{1,0:T(8,128)(2,1)S(1)} %get-tuple-element.12.weights_ref, ...), custom_call_target="tpu_custom_call" | custom-call | tf_op jit(solution)/shard_map/pallas_call | solution.py:380
Async XLA Ops:
  0.6 1.1 %copy-start = (bf16[64,3,4,4,128]{4,3,2,1,0:T(4,128)(2,1)S(1)}, bf16[64,3,4,4,128]{4,3,2,1,0:T(4,128)(2,1)}, u32[]{:S(2)}) copy-start(bf16[64,3,4,4,128]{4,3,2,1,0:T(4,128)(2,1)} %param.5) | copy-start | bytes 2359300
  1.8 1.1 %copy-start.1 = (bf16[63,3,4,4,128]{4,3,2,1,0:T(4,128)(2,1)S(1)}, bf16[63,3,4,4,128]{4,3,2,1,0:T(4,128)(2,1)}, u32[]{:S(2)}) copy-start(bf16[63,3,4,4,128]{4,3,2,1,0:T(4,128)(2,1)} %param.7) | copy-start | bytes 2322436
  2.9 0.9 %copy-start.2 = (f32[3,8,8,128]{3,2,1,0:T(8,128)S(1)}, f32[3,8,8,128]{3,2,1,0:T(8,128)}, u32[]{:S(2)}) copy-start(f32[3,8,8,128]{3,2,1,0:T(8,128)} %v_ref.1) | copy-start | bytes 294916
  3.8 0.7 %copy-start.3 = (f32[64]{0:T(128)S(1)}, f32[64]{0:T(128)}, u32[]{:S(2)}) copy-start(f32[64]{0:T(128)} %strength_ref.1) | copy-start | bytes 772

commit v3 on v2

--- a/solution.py
+++ b/solution.py
@@ -24,9 +24,10 @@
 
 
 def kernel(
-    sizes, rows_total, v_ref, strength_ref, old_hbm, snap_hbm,
-    field_ref, level_ref, weights_ref, earlier_ref,
-    old_ref, snap_ref, wide_ref, load_sem,
+    sizes, rows_total, v_hbm, strength_hbm, old_hbm, snap_hbm,
+    field_hbm, level_ref, weights_ref, whole_hbm,
+    field_ref, earlier_ref, store_sem,
+    v_ref, strength_ref, old_ref, snap_ref, wide_ref, load_sem,
     stage, zsend, xsend, yrecv, zrecv, xrecv,
     gram_ref, part_ref, plane_ref, line_ref, full_ref,
     cross_send, cross_plane, cross_mid, cross_line,
@@ -56,6 +57,8 @@
     x_ways = 1 if n_grp == 2 else 2
 
     loads = [
+        pltpu.make_async_copy(v_hbm, v_ref, load_sem.at[2]),
+        pltpu.make_async_copy(strength_hbm, strength_ref, load_sem.at[3]),
         pltpu.make_async_copy(old_hbm, old_ref, load_sem.at[0]),
         pltpu.make_async_copy(snap_hbm, snap_ref, load_sem.at[1]),
     ]
@@ -100,39 +103,51 @@
     high_lane = lane == line + nx // 2
 
     def send(s, f):
-        stage[s] = f
+        copies = halo_copies(s)
         zsend[s, 0] = f[:, :, nz - 1, :]
         zsend[s, 1] = f[:, :, 0, :]
+        for copy in copies[2:4]:
+            copy.start()
+        stage[s] = f
+        for copy in copies[:2]:
+            copy.start()
         flat = f.reshape(lines, nz, nx)
         packed = jnp.where(low_lane, flat[:, :, 0:1], 0.0)
-        packed = packed + jnp.where(high_lane, flat[:, :, nx - 1 : nx], 0.0)
+        packed = jnp.where(high_lane, flat[:, :, nx - 1 : nx], packed)
         xsend[s] = jnp.sum(packed, axis=0)
-        copies = halo_copies(s)
-        for copy in copies:
+        for copy in copies[4:]:
             copy.start()
         return copies
 
     def stepped(s, f, copies):
-        for copy in copies:
+        flat = f.reshape(lines, nz, nx)
+        left, right = pltpu.roll(flat, 1, 2), pltpu.roll(flat, nx - 1, 2)
+        below, above = pltpu.roll(flat, 1, 1), pltpu.roll(flat, nz - 1, 1)
+        for copy in copies[:2]:
             copy.wait_recv()
-        flat = f.reshape(lines, nz, nx)
         bottom = jnp.where(gy == 0, 0.0, yrecv[s, 0])
         upper = jnp.where(gy == n_gy - 1, 0.0, yrecv[s, 1])
         y_minus = jnp.concatenate([bottom[:, None], f[:, :-1]], axis=1)
         y_plus = jnp.concatenate([f[:, 1:], upper[:, None]], axis=1)
-        z_low = zrecv[s, 0].reshape(lines, 1, nx)
-        z_high = zrecv[s, 1].reshape(lines, 1, nx)
-        z_minus = jnp.where(row == 0, z_low, pltpu.roll(flat, 1, 1)).reshape(f.shape)
-        z_plus = jnp.where(row == nz - 1, z_high, pltpu.roll(flat, nz - 1, 1)).reshape(f.shape)
+        carried = f[1][None] * (y_plus - y_minus) * 0.5
+        spread = y_plus + y_minus - 6.0 * f
+        for copy in copies[4:]:
+            copy.wait_recv()
         from_left, from_right = xrecv[s, 0], xrecv[s, x_ways - 1]
         x_low = jnp.sum(jnp.where(high_lane, from_left[None], 0.0), axis=2, keepdims=True)
         x_high = jnp.sum(jnp.where(low_lane, from_right[None], 0.0), axis=2, keepdims=True)
-        x_minus = jnp.where(lane == 0, x_low, pltpu.roll(flat, 1, 2)).reshape(f.shape)
-        x_plus = jnp.where(lane == nx - 1, x_high, pltpu.roll(flat, nx - 1, 2)).reshape(f.shape)
-        carried = f[0][None] * (x_plus - x_minus) * 0.5
-        carried = carried + f[1][None] * (y_plus - y_minus) * 0.5
+        x_minus = jnp.where(lane == 0, x_low, left).reshape(f.shape)
+        x_plus = jnp.where(lane == nx - 1, x_high, right).reshape(f.shape)
+        carried = carried + f[0][None] * (x_plus - x_minus) * 0.5
+        spread = spread + (x_plus + x_minus)
+        for copy in copies[2:4]:
+            copy.wait_recv()
+        z_low = zrecv[s, 0].reshape(lines, 1, nx)
+        z_high = zrecv[s, 1].reshape(lines, 1, nx)
+        z_minus = jnp.where(row == 0, z_low, below).reshape(f.shape)
+        z_plus = jnp.where(row == nz - 1, z_high, above).reshape(f.shape)
         carried = carried + f[2][None] * (z_plus - z_minus) * 0.5
-        spread = x_plus + x_minus + y_plus + y_minus + z_plus + z_minus - 6.0 * f
+        spread = spread + (z_plus + z_minus)
         return f + time_step * (viscosity * spread - carried)
 
     def scatter_copy(i):
@@ -175,27 +190,32 @@
 
     modes, count = old_ref.shape[0], old_ref.shape[1]
 
-    def flatten():
-        for load in loads:
+    def flatten_old():
+        for load in loads[1:]:
             load.wait()
 
         def scale_row(r, carry):
             wide_ref[pl.ds(r * count, count), :] = strength_ref[r] * old_ref[r].astype(jnp.float32)
             return carry
 
+        lax.fori_loop(0, modes, scale_row, 0, unroll=8)
+
+    def flatten_snapshots():
         def copy_row(r, carry):
             wide_ref[pl.ds((r + modes) * count, count), :] = snap_ref[r].astype(jnp.float32)
             return carry
 
-        lax.fori_loop(0, modes, scale_row, 0, unroll=8)
         lax.fori_loop(0, snap_ref.shape[0], copy_row, 0, unroll=7)
         wide_ref[pl.ds((ranks - 1) * count, count), :] = jnp.zeros((count, nx), jnp.float32)
-        for b in range(count):
+        take_columns(0, count // 2)
+
+    def take_columns(first, stop):
+        for b in range(first, stop):
             column = wide_ref[pl.ds(b, ranks, stride=count), :]
             earlier_ref[:, b * nx : (b + 1) * nx] = column.astype(jnp.bfloat16)
 
     def begin_gram():
-        flatten()
+        take_columns(count // 2, count)
         earlier = earlier_ref[...]
         gram = lax.dot_general(
             earlier, earlier, (((1,), (1,)), ((), ())), preferred_element_type=jnp.float32
@@ -216,7 +236,8 @@
         full_ref[me] = jnp.sum(line_ref[...], axis=0)
         each(n_plane - 1, lambda i: gather_copy(i).start())
 
-    between = {0: begin_gram, 2: add_plane, 3: add_line}
+    between = {0: flatten_old, 1: flatten_snapshots, 2: begin_gram, 3: add_plane, 4: add_line}
+    loads[0].wait()
     base = v_ref[...]
     f = base
     for s in range(STAGES):
@@ -232,6 +253,8 @@
             f = base / 3.0 + 2.0 / 3.0 * moved
             base = f
     field_ref[...] = f
+    field_store = pltpu.make_async_copy(field_ref, field_hbm, store_sem.at[0])
+    field_store.start()
 
     blocks = [(c, y, z) for c in range(comps) for y in range(0, ny, 2) for z in range(0, nz, 2)]
 
@@ -258,6 +281,8 @@
         columns = slice(b * nx, (b + 1) * nx)
         rows = earlier_ref[tail, columns].astype(jnp.float32)
         earlier_ref[tail, columns] = jnp.where(last, newest_block(b), rows).astype(jnp.bfloat16)
+    whole_store = pltpu.make_async_copy(earlier_ref, whole_hbm, store_sem.at[1])
+    whole_store.start()
     wait_plane(full_ref, crecv_sem)
     wait_plane(cross_plane, drecv_sem)
     cross_mid[...] = jnp.sum(cross_plane[...], axis=0)
@@ -273,20 +298,36 @@
     scale = jnp.sqrt(jnp.sum(gram * gram, keepdims=True))
     level = gram / scale
     ident = jnp.where(square_row == square_col, 1.0, 0.0)
-    dot = functools.partial(
-        jnp.dot, precision=lax.Precision.HIGHEST, preferred_element_type=jnp.float32
-    )
-    inverse = ident
+
+    def split(a):
+        coarse = a.astype(jnp.bfloat16)
+        return coarse, (a - coarse.astype(jnp.float32)).astype(jnp.bfloat16)
+
+    def dot(left, right):
+        terms = jnp.concatenate(right, axis=1)
+        both = jnp.dot(
+            jnp.concatenate(left, axis=1),
+            jnp.concatenate([terms, terms], axis=0),
+            preferred_element_type=jnp.float32,
+        )
+        return both[:, :ranks] + both[:, ranks:]
+
+    inverse, inverse_split = ident, None
     for repeat in range(NS_ITERS):
-        product = level if repeat == 0 else dot(inverse, level)
+        level_split = split(level)
+        product = level if repeat == 0 else dot(inverse_split, level_split)
         factor = 1.5 * ident - 0.5 * product
-        level = dot(level, factor)
-        inverse = factor if repeat == 0 else dot(factor, inverse)
+        factor_split = split(factor)
+        inverse = factor if repeat == 0 else dot(factor_split, inverse_split)
+        level = dot(level_split, factor_split)
+        inverse_split = split(inverse)
     level_ref[...] = level
     factor = jnp.sqrt(jnp.full((1, 1), rows_total, jnp.float32)) / jnp.sqrt(scale)
     weights = (inverse * factor).astype(jnp.bfloat16)
     weights_ref[...] = weights
 
+    field_store.wait()
+    whole_store.wait()
     for s in range(STAGES):
         for copy in halo_copies(s):
             copy.wait_send()
@@ -297,21 +338,44 @@
     each(n_gz - 1, lambda i: cross_line_copy(i).wait_send())
 
 
-def rotate(field_in, level_in, weights_ref, whole_ref, field_ref, level_ref, basis_ref, wide_ref):
-    field_ref[...] = field_in[...]
-    level_ref[...] = level_in[...]
+def rotate(
+    field_in, level_in, weights_in, whole_in, field_out, level_out, basis_out,
+    weights_ref, whole_ref, wide_ref, basis_ref, pass_sem, load_sem, store_sem,
+):
     ranks, count, nx = basis_ref.shape
+    parts = load_sem.shape[0] - 1
+    width = count // parts * nx
+    loads = [pltpu.make_async_copy(weights_in, weights_ref, load_sem.at[parts])]
+    for p in range(parts):
+        columns = (slice(None), pl.ds(p * width, width))
+        loads.append(pltpu.make_async_copy(whole_in.at[columns], whole_ref.at[columns], load_sem.at[p]))
+    passes = [
+        pltpu.make_async_copy(field_in, field_out, pass_sem.at[0]),
+        pltpu.make_async_copy(level_in, level_out, pass_sem.at[1]),
+    ]
+    for copy in loads + passes:
+        copy.start()
+    loads[0].wait()
     weights = weights_ref[...]
-    for b in range(count):
-        wide_ref[pl.ds(b, ranks, stride=count), :] = jnp.dot(
-            weights, whole_ref[:, b * nx : (b + 1) * nx], preferred_element_type=jnp.float32
-        )
-
-    def write(r, carry):
-        basis_ref[r] = wide_ref[pl.ds(r * count, count), :].astype(jnp.bfloat16)
-        return carry
-
-    lax.fori_loop(0, ranks, write, 0, unroll=8)
+    for p in range(parts):
+        loads[p + 1].wait()
+        for b in range(p * count // parts, (p + 1) * count // parts, 2):
+            pair = jnp.dot(
+                weights, whole_ref[:, b * nx : (b + 2) * nx], preferred_element_type=jnp.float32
+            )
+            wide_ref[pl.ds(b, ranks, stride=count), :] = pair[:, :nx]
+            wide_ref[pl.ds(b + 1, ranks, stride=count), :] = pair[:, nx:]
+    pieces = store_sem.shape[0]
+    depth = ranks // pieces
+    stores = []
+    for p in range(pieces):
+        rows = pl.ds(p * depth, depth)
+        piece = wide_ref[pl.ds(p * depth * count, depth * count), :].astype(jnp.bfloat16)
+        basis_ref[rows] = piece.reshape(depth, count, nx)
+        stores.append(pltpu.make_async_copy(basis_ref.at[rows], basis_out.at[rows], store_sem.at[p]))
+        stores[-1].start()
+    for copy in passes + stores:
+        copy.wait()
 
 
 def local(velocity, basis_old, strength, snapshots):
@@ -329,6 +393,7 @@
     f32 = jnp.float32
     dma = pltpu.SemaphoreType.DMA
     vmem = pl.BlockSpec(memory_space=pltpu.VMEM)
+    hbm = pl.BlockSpec(memory_space=pltpu.HBM)
     field, level, weights, whole = pl.pallas_call(
         functools.partial(kernel, sizes, float(length * n_plane * n_gz)),
         out_shape=(
@@ -338,17 +403,22 @@
             jax.ShapeDtypeStruct((ranks, length), jnp.bfloat16),
         ),
         in_specs=[
-            vmem,
-            pl.BlockSpec(memory_space=pltpu.SMEM),
-            pl.BlockSpec(memory_space=pltpu.HBM),
-            pl.BlockSpec(memory_space=pltpu.HBM),
+            hbm,
+            hbm,
+            hbm,
+            hbm,
         ],
-        out_specs=(vmem, vmem, vmem, vmem),
+        out_specs=(hbm, vmem, vmem, hbm),
         scratch_shapes=[
+            pltpu.VMEM(velocity.shape, f32),
+            pltpu.VMEM((ranks, length), jnp.bfloat16),
+            dma((2,)),
+            pltpu.VMEM(velocity.shape, f32),
+            pltpu.SMEM((modes,), f32),
             pltpu.VMEM((modes, count, nx), jnp.bfloat16),
             pltpu.VMEM((earlier_count, count, nx), jnp.bfloat16),
             pltpu.VMEM((ranks * count, nx), f32),
-            dma((2,)),
+            dma((4,)),
             pltpu.VMEM((STAGES,) + velocity.shape, f32),
             pltpu.VMEM((STAGES, 2, comps, ny, nx), f32),
             pltpu.VMEM((STAGES, nz, nx), f32),
@@ -374,7 +444,7 @@
             dma((n_gz,)), dma((n_gz,)),
         ],
         compiler_params=pltpu.CompilerParams(
-            collective_id=0, has_side_effects=True, vmem_limit_bytes=24 * 1024 * 1024
+            collective_id=0, has_side_effects=True, vmem_limit_bytes=56 * 1024 * 1024
         ),
     )(velocity, strength, basis_old.reshape(modes, count, nx), snapshots.reshape(earlier_count, count, nx))
     field, level, basis_new = pl.pallas_call(
@@ -384,10 +454,18 @@
             jax.ShapeDtypeStruct((ranks, ranks), f32),
             jax.ShapeDtypeStruct((ranks, count, nx), jnp.bfloat16),
         ),
-        in_specs=[vmem, vmem, vmem, vmem],
-        out_specs=(vmem, vmem, vmem),
-        scratch_shapes=[pltpu.VMEM((ranks * count, nx), f32)],
-        compiler_params=pltpu.CompilerParams(vmem_limit_bytes=16 * 1024 * 1024),
+        in_specs=[hbm] * 4,
+        out_specs=(hbm,) * 3,
+        scratch_shapes=[
+            pltpu.VMEM((ranks, ranks), jnp.bfloat16),
+            pltpu.VMEM((ranks, length), jnp.bfloat16),
+            pltpu.VMEM((ranks * count, nx), f32),
+            pltpu.VMEM((ranks, count, nx), jnp.bfloat16),
+            dma((2,)),
+            dma((5,)),
+            dma((4,)),
+        ],
+        compiler_params=pltpu.CompilerParams(vmem_limit_bytes=56 * 1024 * 1024),
     )(field, level, weights, whole)
     basis_new = basis_new.reshape(ranks, comps, ny // 2, nz // 2, nx)
     return (field, basis_new, level)

time: 49.5 us -> 46.3 us (0.935)
  local copies, waits for them, and re-layouts: 3.8 us -> 0 us
  Pallas kernels: 44.8 us -> 45.5 us
    unnamed x8 -> x0, local copies, waits for them, and re-layouts: 3.8 us -> none
    pallas_call x1, Pallas kernels: 2.78 us -> 6.18 us  [local(): pl.pallas_call(rotate, out_shape=(jax.ShapeDtypeStruct(velocity.shape, f3...]
    pallas_call x1, Pallas kernels: 42 us -> 39.4 us  [local(): pl.pallas_call(functools.partial(kernel, sizes, float(length * n_plane *...]
where the time goes in v3:
time: 46.3 us; the launch traced here: 46.2 us
  Pallas kernels  45.5 us (98%)
  between operations  0.64 us (1%)
    pallas_call x1, Pallas kernels, local(): pl.pallas_call(functools.partial(kernel, sizes, float(length * n_plane *...  39.4 us
    pallas_call x1, Pallas kernels, local(): pl.pallas_call(rotate, out_shape=(jax.ShapeDtypeStruct(velocity.shape, f3...  6.18 us

profile of v3, /device:TPU:0, one launch (start us, length us, event | category | flops | bytes accessed | tf_op | source)
XLA Modules:
  0.0 46.2 jit_solution(10345172262494263005)
XLA Ops:
  0.6 39.4 %shard_map.67 = (f32[3,8,8,128]{3,2,1,0:T(8,128)}, f32[128,128]{1,0:T(8,128)}, bf16[128,128]{1,0:T(8,128)(2,1)}, bf16[128,6144]{1,0:T(8,128)(2,1)}) custom-call(f32[3,8,8,128]{3,2,1,0:T(8,128)} %v_hbm.1, f32[64]{0:T(128)} %strength_hbm.1, bf16[64,48,128]{2,1,0:T(8,128)(2,1)} %bitcast.3, bf16[63,48,128]{2,1,0:T(8,128)(2,1)} %bitcast.4), custom_call_target="tpu_custom_call" | custom-call | tf_op jit(solution)/shard_map/pallas_call | solution.py:397
  40.0 6.2 %shard_map.68 = (f32[3,8,8,128]{3,2,1,0:T(8,128)}, f32[128,128]{1,0:T(8,128)}, bf16[128,48,128]{2,1,0:T(8,128)(2,1)}) custom-call(f32[3,8,8,128]{3,2,1,0:T(8,128)} %get-tuple-element.10.field_in, f32[128,128]{1,0:T(8,128)} %get-tuple-element.11.level_in, bf16[128,128]{1,0:T(8,128)(2,1)} %get-tuple-element.12.weights_in, ...), custom_call_target="tpu_custom_call" | custom-call | tf_op jit(solution)/shard_map/pallas_call | solution.py:450

commit v4 on v3

--- a/solution.py
+++ b/solution.py
@@ -316,10 +316,10 @@
     for repeat in range(NS_ITERS):
         level_split = split(level)
         product = level if repeat == 0 else dot(inverse_split, level_split)
-        factor = 1.5 * ident - 0.5 * product
-        factor_split = split(factor)
-        inverse = factor if repeat == 0 else dot(factor_split, inverse_split)
-        level = dot(level_split, factor_split)
+        product_split = split(product)
+        moved = product if repeat == 0 else dot(product_split, inverse_split)
+        inverse = 1.5 * inverse - 0.5 * moved
+        level = 1.5 * level - 0.5 * dot(level_split, product_split)
         inverse_split = split(inverse)
     level_ref[...] = level
     factor = jnp.sqrt(jnp.full((1, 1), rows_total, jnp.float32)) / jnp.sqrt(scale)
@@ -340,7 +340,7 @@
 
 def rotate(
     field_in, level_in, weights_in, whole_in, field_out, level_out, basis_out,
-    weights_ref, whole_ref, wide_ref, basis_ref, pass_sem, load_sem, store_sem,
+    field_ref, level_ref, weights_ref, whole_ref, wide_ref, basis_ref, pass_sem, load_sem, store_sem,
 ):
     ranks, count, nx = basis_ref.shape
     parts = load_sem.shape[0] - 1
@@ -349,11 +349,15 @@
     for p in range(parts):
         columns = (slice(None), pl.ds(p * width, width))
         loads.append(pltpu.make_async_copy(whole_in.at[columns], whole_ref.at[columns], load_sem.at[p]))
+    arrivals = [
+        pltpu.make_async_copy(field_in, field_ref, pass_sem.at[0]),
+        pltpu.make_async_copy(level_in, level_ref, pass_sem.at[1]),
+    ]
     passes = [
-        pltpu.make_async_copy(field_in, field_out, pass_sem.at[0]),
-        pltpu.make_async_copy(level_in, level_out, pass_sem.at[1]),
+        pltpu.make_async_copy(field_ref, field_out, pass_sem.at[2]),
+        pltpu.make_async_copy(level_ref, level_out, pass_sem.at[3]),
     ]
-    for copy in loads + passes:
+    for copy in loads + arrivals:
         copy.start()
     loads[0].wait()
     weights = weights_ref[...]
@@ -365,6 +369,9 @@
             )
             wide_ref[pl.ds(b, ranks, stride=count), :] = pair[:, :nx]
             wide_ref[pl.ds(b + 1, ranks, stride=count), :] = pair[:, nx:]
+    for arrival, copy in zip(arrivals, passes):
+        arrival.wait()
+        copy.start()
     pieces = store_sem.shape[0]
     depth = ranks // pieces
     stores = []
@@ -457,11 +464,13 @@
         in_specs=[hbm] * 4,
         out_specs=(hbm,) * 3,
         scratch_shapes=[
+            pltpu.VMEM(velocity.shape, f32),
+            pltpu.VMEM((ranks, ranks), f32),
             pltpu.VMEM((ranks, ranks), jnp.bfloat16),
             pltpu.VMEM((ranks, length), jnp.bfloat16),
             pltpu.VMEM((ranks * count, nx), f32),
             pltpu.VMEM((ranks, count, nx), jnp.bfloat16),
-            dma((2,)),
+            dma((4,)),
             dma((5,)),
             dma((4,)),
         ],

time: 46.3 us -> 44 us (0.950)
  Pallas kernels: 45.5 us -> 43.2 us
    pallas_call x1, Pallas kernels: 6.18 us -> 3.77 us  [local(): pl.pallas_call(rotate, out_shape=(jax.ShapeDtypeStruct(velocity.shape, f3...]
where the time goes in v4:
time: 44 us; the launch traced here: 43.8 us
  Pallas kernels  43.2 us (98%)
  between operations  0.64 us (1%)
    pallas_call x1, Pallas kernels, local(): pl.pallas_call(functools.partial(kernel, sizes, float(length * n_plane *...  39.4 us
    pallas_call x1, Pallas kernels, local(): pl.pallas_call(rotate, out_shape=(jax.ShapeDtypeStruct(velocity.shape, f3...  3.77 us

profile of v4, /device:TPU:0, one launch (start us, length us, event | category | flops | bytes accessed | tf_op | source)
XLA Modules:
  0.0 43.8 jit_solution(8601120811030560552)
XLA Ops:
  0.6 39.4 %shard_map.67 = (f32[3,8,8,128]{3,2,1,0:T(8,128)}, f32[128,128]{1,0:T(8,128)}, bf16[128,128]{1,0:T(8,128)(2,1)}, bf16[128,6144]{1,0:T(8,128)(2,1)}) custom-call(f32[3,8,8,128]{3,2,1,0:T(8,128)} %v_hbm.1, f32[64]{0:T(128)} %strength_hbm.1, bf16[64,48,128]{2,1,0:T(8,128)(2,1)} %bitcast.3, bf16[63,48,128]{2,1,0:T(8,128)(2,1)} %bitcast.4), custom_call_target="tpu_custom_call" | custom-call | tf_op jit(solution)/shard_map/pallas_call | solution.py:404
  40.0 3.8 %shard_map.68 = (f32[3,8,8,128]{3,2,1,0:T(8,128)}, f32[128,128]{1,0:T(8,128)}, bf16[128,48,128]{2,1,0:T(8,128)(2,1)}) custom-call(f32[3,8,8,128]{3,2,1,0:T(8,128)} %get-tuple-element.10.field_in, f32[128,128]{1,0:T(8,128)} %get-tuple-element.11.level_in, bf16[128,128]{1,0:T(8,128)(2,1)} %get-tuple-element.12.weights_in, ...), custom_call_target="tpu_custom_call" | custom-call | tf_op jit(solution)/shard_map/pallas_call | solution.py:457

commit v5 on v4

--- a/solution.py
+++ b/solution.py
@@ -9,6 +9,7 @@
 
 NS_ITERS = 8
 STAGES = 6
+DIRECT_LIMIT = 64
 MESH = pl.DeviceIdType.MESH
 
 time_step = 0.1
@@ -16,7 +17,7 @@
 
 
 def each(count, body):
-    if count <= 8:
+    if count <= 32:
         for i in range(count):
             body(i)
     else:
@@ -47,6 +48,16 @@
         peer = lax.rem(me + offset, n_plane)
         return peer, {"grp": peer // n_gy, "gy": lax.rem(peer, n_gy)}
 
+    everyone = n_plane * n_gz
+    direct = everyone <= DIRECT_LIMIT
+    my_place = me * n_gz + gz
+
+    def any_id(offset):
+        peer = lax.rem(my_place + offset, everyone)
+        plane = peer // n_gz
+        target = {"grp": plane // n_gy, "gy": lax.rem(plane, n_gy), "gz": lax.rem(peer, n_gz)}
+        return peer, target
+
     def line_id(offset):
         peer = lax.rem(gz + offset, n_gz)
         return peer, {"gz": peer}
@@ -72,9 +83,16 @@
     def greet_line(i):
         pl.semaphore_signal(barrier, inc=1, device_id=line_id(i + 1)[1], device_id_type=MESH)
 
-    each(n_plane - 1, greet_plane)
-    each(n_gz - 1, greet_line)
-    pl.semaphore_wait(barrier, n_plane + n_gz - 2)
+    def greet_any(i):
+        pl.semaphore_signal(barrier, inc=1, device_id=any_id(i + 1)[1], device_id_type=MESH)
+
+    if direct:
+        each(everyone - 1, greet_any)
+        greeted = everyone - 1
+    else:
+        each(n_plane - 1, greet_plane)
+        each(n_gz - 1, greet_line)
+        greeted = n_plane + n_gz - 2
 
     def remote(src, dst, send_sem, recv_sem, target):
         return pltpu.make_async_remote_copy(
@@ -104,17 +122,27 @@
 
     def send(s, f):
         copies = halo_copies(s)
+        flat = f.reshape(lines, nz, nx)
+
+        def pack_x():
+            packed = jnp.where(low_lane, flat[:, :, 0:1], 0.0)
+            packed = jnp.where(high_lane, flat[:, :, nx - 1 : nx], packed)
+            xsend[s] = jnp.sum(packed, axis=0)
+
         zsend[s, 0] = f[:, :, nz - 1, :]
         zsend[s, 1] = f[:, :, 0, :]
+        if s == 0:
+            stage[s] = f
+            pack_x()
+            pl.semaphore_wait(barrier, greeted)
         for copy in copies[2:4]:
             copy.start()
-        stage[s] = f
+        if s > 0:
+            stage[s] = f
         for copy in copies[:2]:
             copy.start()
-        flat = f.reshape(lines, nz, nx)
-        packed = jnp.where(low_lane, flat[:, :, 0:1], 0.0)
-        packed = jnp.where(high_lane, flat[:, :, nx - 1 : nx], packed)
-        xsend[s] = jnp.sum(packed, axis=0)
+        if s > 0:
+            pack_x()
         for copy in copies[4:]:
             copy.start()
         return copies
@@ -174,6 +202,19 @@
         _, target = line_id(i + 1)
         return remote(cross_mid, cross_line.at[gz], esend_sem.at[i], erecv_sem.at[gz], target)
 
+    def cross_any_copy(i):
+        _, target = any_id(i + 1)
+        return remote(
+            cross_send, cross_plane.at[my_place], dsend_sem.at[i], drecv_sem.at[my_place], target
+        )
+
+    def wait_any(buffer, sem):
+        def body(i):
+            peer, target = any_id(i + 1)
+            remote(buffer.at[peer], buffer.at[peer], sem.at[peer], sem.at[peer], target).wait_recv()
+
+        each(everyone - 1, body)
+
     def wait_plane(buffer, sem):
         def body(i):
             peer, target = plane_id(i + 1)
@@ -272,9 +313,13 @@
     square_col = lax.broadcasted_iota(jnp.int32, (ranks, ranks), 1)
     total = jnp.where(lax.broadcasted_iota(jnp.int32, (ranks, nx), 0) == ranks - 1, own, total)
     cross = jnp.sum(total.T, axis=0, keepdims=True)
-    cross_send[...] = jnp.broadcast_to(cross, cross_send.shape)
-    cross_plane[me] = cross_send[...]
-    each(n_plane - 1, lambda i: cross_plane_copy(i).start())
+    cross_send[...] = cross
+    if direct:
+        cross_plane[my_place] = cross
+        each(everyone - 1, lambda i: cross_any_copy(i).start())
+    else:
+        cross_plane[me] = cross
+        each(n_plane - 1, lambda i: cross_plane_copy(i).start())
     tail = slice(ranks - 16, ranks)
     last = lax.broadcasted_iota(jnp.int32, (16, nx), 0) == 15
     for b in range(len(blocks)):
@@ -284,12 +329,16 @@
     whole_store = pltpu.make_async_copy(earlier_ref, whole_hbm, store_sem.at[1])
     whole_store.start()
     wait_plane(full_ref, crecv_sem)
-    wait_plane(cross_plane, drecv_sem)
-    cross_mid[...] = jnp.sum(cross_plane[...], axis=0)
-    cross_line[gz] = cross_mid[...]
-    each(n_gz - 1, lambda i: cross_line_copy(i).start())
-    wait_line(cross_line, erecv_sem)
-    cross = jnp.sum(cross_line[...], axis=0)[0:1]
+    if direct:
+        wait_any(cross_plane, drecv_sem)
+        cross = jnp.sum(cross_plane[...], axis=0)
+    else:
+        wait_plane(cross_plane, drecv_sem)
+        cross_mid[...] = jnp.sum(cross_plane[...], axis=0)
+        cross_line[gz] = cross_mid[...]
+        each(n_gz - 1, lambda i: cross_line_copy(i).start())
+        wait_line(cross_line, erecv_sem)
+        cross = jnp.sum(cross_line[...], axis=0)
     cross = jnp.broadcast_to(cross, (ranks, ranks))
 
     gram = full_ref[...].reshape(ranks, ranks)
@@ -334,8 +383,11 @@
     each(n_plane - 1, lambda i: scatter_copy(i).wait_send())
     each(n_gz - 1, lambda i: line_copy(i).wait_send())
     each(n_plane - 1, lambda i: gather_copy(i).wait_send())
-    each(n_plane - 1, lambda i: cross_plane_copy(i).wait_send())
-    each(n_gz - 1, lambda i: cross_line_copy(i).wait_send())
+    if direct:
+        each(everyone - 1, lambda i: cross_any_copy(i).wait_send())
+    else:
+        each(n_plane - 1, lambda i: cross_plane_copy(i).wait_send())
+        each(n_gz - 1, lambda i: cross_line_copy(i).wait_send())
 
 
 def rotate(
@@ -397,6 +449,8 @@
     length = count * nx
     share = ranks // n_plane
     assert share * n_plane == ranks
+    everyone = n_plane * n_gz
+    senders = everyone if everyone <= DIRECT_LIMIT else n_plane
     f32 = jnp.float32
     dma = pltpu.SemaphoreType.DMA
     vmem = pl.BlockSpec(memory_space=pltpu.VMEM)
@@ -437,17 +491,17 @@
             pltpu.VMEM((n_plane, share, ranks), f32),
             pltpu.VMEM((n_gz, share, ranks), f32),
             pltpu.VMEM((n_plane, share, ranks), f32),
-            pltpu.VMEM((8, ranks), f32),
-            pltpu.VMEM((n_plane, 8, ranks), f32),
-            pltpu.VMEM((8, ranks), f32),
-            pltpu.VMEM((n_gz, 8, ranks), f32),
+            pltpu.VMEM((1, ranks), f32),
+            pltpu.VMEM((senders, 1, ranks), f32),
+            pltpu.VMEM((1, ranks), f32),
+            pltpu.VMEM((n_gz, 1, ranks), f32),
             dma((STAGES, 2)), dma((STAGES, 2)),
             dma((STAGES, 2)), dma((STAGES, 2)),
             dma((STAGES, 2)), dma((STAGES, 2)),
             dma((n_plane,)), dma((n_plane,)),
             dma((n_gz,)), dma((n_gz,)),
             dma((n_plane,)), dma((n_plane,)),
-            dma((n_plane,)), dma((n_plane,)),
+            dma((senders,)), dma((senders,)),
             dma((n_gz,)), dma((n_gz,)),
         ],
         compiler_params=pltpu.CompilerParams(

time: 44 us -> 43.4 us (0.986)
  Pallas kernels: 43.2 us -> 42.6 us
    pallas_call x1, Pallas kernels: 39.4 us -> 38.8 us  [local(): pl.pallas_call(functools.partial(kernel, sizes, float(length * n_plane *...]
where the time goes in v5:
time: 43.4 us; the launch traced here: 43.2 us
  Pallas kernels  42.6 us (98%)
  between operations  0.64 us (1%)
    pallas_call x1, Pallas kernels, local(): pl.pallas_call(functools.partial(kernel, sizes, float(length * n_plane *...  38.8 us
    pallas_call x1, Pallas kernels, local(): pl.pallas_call(rotate, out_shape=(jax.ShapeDtypeStruct(velocity.shape, f3...  3.78 us

profile of v5, /device:TPU:0, one launch (start us, length us, event | category | flops | bytes accessed | tf_op | source)
XLA Modules:
  0.0 43.2 jit_solution(7065656434284036142)
XLA Ops:
  0.6 38.8 %shard_map.67 = (f32[3,8,8,128]{3,2,1,0:T(8,128)}, f32[128,128]{1,0:T(8,128)}, bf16[128,128]{1,0:T(8,128)(2,1)}, bf16[128,6144]{1,0:T(8,128)(2,1)}) custom-call(f32[3,8,8,128]{3,2,1,0:T(8,128)} %v_hbm.1, f32[64]{0:T(128)} %strength_hbm.1, bf16[64,48,128]{2,1,0:T(8,128)(2,1)} %bitcast.3, bf16[63,48,128]{2,1,0:T(8,128)(2,1)} %bitcast.4), custom_call_target="tpu_custom_call" | custom-call | tf_op jit(solution)/shard_map/pallas_call | solution.py:458
  39.5 3.8 %shard_map.68 = (f32[3,8,8,128]{3,2,1,0:T(8,128)}, f32[128,128]{1,0:T(8,128)}, bf16[128,48,128]{2,1,0:T(8,128)(2,1)}) custom-call(f32[3,8,8,128]{3,2,1,0:T(8,128)} %get-tuple-element.10.field_in, f32[128,128]{1,0:T(8,128)} %get-tuple-element.11.level_in, bf16[128,128]{1,0:T(8,128)(2,1)} %get-tuple-element.12.weights_in, ...), custom_call_target="tpu_custom_call" | custom-call | tf_op jit(solution)/shard_map/pallas_call | solution.py:511

commit v6 on v5

--- a/solution.py
+++ b/solution.py
@@ -29,7 +29,7 @@
     field_hbm, level_ref, weights_ref, whole_hbm,
     field_ref, earlier_ref, store_sem,
     v_ref, strength_ref, old_ref, snap_ref, wide_ref, load_sem,
-    stage, zsend, xsend, yrecv, zrecv, xrecv,
+    rows_ref, stage, zsend, xsend, yrecv, zrecv, xrecv,
     gram_ref, part_ref, plane_ref, line_ref, full_ref,
     cross_send, cross_plane, cross_mid, cross_line,
     ysend_sem, yrecv_sem, zsend_sem, zrecv_sem, xsend_sem, xrecv_sem,
@@ -115,22 +115,23 @@
         return copies
 
     lane = lax.broadcasted_iota(jnp.int32, (lines, nz, nx), 2)
-    line = lax.broadcasted_iota(jnp.int32, (lines, nz, nx), 0)
-    row = lax.broadcasted_iota(jnp.int32, (lines, nz, nx), 1)
-    low_lane = lane == line
-    high_lane = lane == line + nx // 2
+    flat_lane = lax.broadcasted_iota(jnp.int32, (nz, nx), 1)
+    pair = flat_lane // 2
+    even = flat_lane % 2 == 0
 
     def send(s, f):
         copies = halo_copies(s)
         flat = f.reshape(lines, nz, nx)
 
         def pack_x():
-            packed = jnp.where(low_lane, flat[:, :, 0:1], 0.0)
-            packed = jnp.where(high_lane, flat[:, :, nx - 1 : nx], packed)
-            xsend[s] = jnp.sum(packed, axis=0)
-
-        zsend[s, 0] = f[:, :, nz - 1, :]
-        zsend[s, 1] = f[:, :, 0, :]
+            packed = jnp.zeros((nz, nx), jnp.float32)
+            for k in range(lines):
+                packed = jnp.where(pair == k, pltpu.roll(flat[k], 2 * k + 1, 1), packed)
+            xsend[s] = packed
+
+        rows_ref[0] = f.reshape(lines * nz, nx)
+        zsend[s, 0] = rows_ref[0, pl.ds(nz - 1, lines, stride=nz), :]
+        zsend[s, 1] = rows_ref[0, pl.ds(0, lines, stride=nz), :]
         if s == 0:
             stage[s] = f
             pack_x()
@@ -150,7 +151,8 @@
     def stepped(s, f, copies):
         flat = f.reshape(lines, nz, nx)
         left, right = pltpu.roll(flat, 1, 2), pltpu.roll(flat, nx - 1, 2)
-        below, above = pltpu.roll(flat, 1, 1), pltpu.roll(flat, nz - 1, 1)
+        rows_ref[1] = pltpu.roll(flat, 1, 1).reshape(lines * nz, nx)
+        rows_ref[2] = pltpu.roll(flat, nz - 1, 1).reshape(lines * nz, nx)
         for copy in copies[:2]:
             copy.wait_recv()
         bottom = jnp.where(gy == 0, 0.0, yrecv[s, 0])
@@ -162,18 +164,18 @@
         for copy in copies[4:]:
             copy.wait_recv()
         from_left, from_right = xrecv[s, 0], xrecv[s, x_ways - 1]
-        x_low = jnp.sum(jnp.where(high_lane, from_left[None], 0.0), axis=2, keepdims=True)
-        x_high = jnp.sum(jnp.where(low_lane, from_right[None], 0.0), axis=2, keepdims=True)
-        x_minus = jnp.where(lane == 0, x_low, left).reshape(f.shape)
-        x_plus = jnp.where(lane == nx - 1, x_high, right).reshape(f.shape)
+        merged = jnp.where(even, from_left, pltpu.roll(from_right, nx - 2, 1))
+        edges = jnp.stack([pltpu.roll(merged, (nx - 2 * k) % nx, 1) if k else merged for k in range(lines)])
+        x_minus = jnp.where(lane == 0, edges, left).reshape(f.shape)
+        x_plus = jnp.where(lane == nx - 1, edges, right).reshape(f.shape)
         carried = carried + f[0][None] * (x_plus - x_minus) * 0.5
         spread = spread + (x_plus + x_minus)
         for copy in copies[2:4]:
             copy.wait_recv()
-        z_low = zrecv[s, 0].reshape(lines, 1, nx)
-        z_high = zrecv[s, 1].reshape(lines, 1, nx)
-        z_minus = jnp.where(row == 0, z_low, below).reshape(f.shape)
-        z_plus = jnp.where(row == nz - 1, z_high, above).reshape(f.shape)
+        rows_ref[1, pl.ds(0, lines, stride=nz), :] = zrecv[s, 0]
+        rows_ref[2, pl.ds(nz - 1, lines, stride=nz), :] = zrecv[s, 1]
+        z_minus = rows_ref[1].reshape(f.shape)
+        z_plus = rows_ref[2].reshape(f.shape)
         carried = carried + f[2][None] * (z_plus - z_minus) * 0.5
         spread = spread + (z_plus + z_minus)
         return f + time_step * (viscosity * spread - carried)
@@ -480,11 +482,12 @@
             pltpu.VMEM((earlier_count, count, nx), jnp.bfloat16),
             pltpu.VMEM((ranks * count, nx), f32),
             dma((4,)),
+            pltpu.VMEM((3, comps * ny * nz, nx), f32),
             pltpu.VMEM((STAGES,) + velocity.shape, f32),
-            pltpu.VMEM((STAGES, 2, comps, ny, nx), f32),
+            pltpu.VMEM((STAGES, 2, comps * ny, nx), f32),
             pltpu.VMEM((STAGES, nz, nx), f32),
             pltpu.VMEM((STAGES, 2, comps, nz, nx), f32),
-            pltpu.VMEM((STAGES, 2, comps, ny, nx), f32),
+            pltpu.VMEM((STAGES, 2, comps * ny, nx), f32),
             pltpu.VMEM((STAGES, 2, nz, nx), f32),
             pltpu.VMEM((n_plane, share, ranks), f32),
             pltpu.VMEM((share, ranks), f32),

time: 43.4 us -> 43.2 us (level)
  no operation moved by 1% of the time
where the time goes in v6:
time: 43.2 us; the launch traced here: 43 us
  Pallas kernels  42.4 us (98%)
  between operations  0.64 us (1%)
    pallas_call x1, Pallas kernels, local(): pl.pallas_call(functools.partial(kernel, sizes, float(length * n_plane *...  38.6 us
    pallas_call x1, Pallas kernels, local(): pl.pallas_call(rotate, out_shape=(jax.ShapeDtypeStruct(velocity.shape, f3...  3.78 us

profile of v6, /device:TPU:0, one launch (start us, length us, event | category | flops | bytes accessed | tf_op | source)
XLA Modules:
  0.0 43.0 jit_solution(6804589039662055626)
XLA Ops:
  0.6 38.6 %shard_map.67 = (f32[3,8,8,128]{3,2,1,0:T(8,128)}, f32[128,128]{1,0:T(8,128)}, bf16[128,128]{1,0:T(8,128)(2,1)}, bf16[128,6144]{1,0:T(8,128)(2,1)}) custom-call(f32[3,8,8,128]{3,2,1,0:T(8,128)} %v_hbm.1, f32[64]{0:T(128)} %strength_hbm.1, bf16[64,48,128]{2,1,0:T(8,128)(2,1)} %bitcast.3, bf16[63,48,128]{2,1,0:T(8,128)(2,1)} %bitcast.4), custom_call_target="tpu_custom_call" | custom-call | tf_op jit(solution)/shard_map/pallas_call | solution.py:460
  39.3 3.8 %shard_map.68 = (f32[3,8,8,128]{3,2,1,0:T(8,128)}, f32[128,128]{1,0:T(8,128)}, bf16[128,48,128]{2,1,0:T(8,128)(2,1)}) custom-call(f32[3,8,8,128]{3,2,1,0:T(8,128)} %get-tuple-element.10.field_in, f32[128,128]{1,0:T(8,128)} %get-tuple-element.11.level_in, bf16[128,128]{1,0:T(8,128)(2,1)} %get-tuple-element.12.weights_in, ...), custom_call_target="tpu_custom_call" | custom-call | tf_op jit(solution)/shard_map/pallas_call | solution.py:514

commit v7 on v6

--- a/solution.py
+++ b/solution.py
@@ -232,29 +232,30 @@
         each(n_gz - 1, body)
 
     modes, count = old_ref.shape[0], old_ref.shape[1]
+    pitch = wide_ref.shape[0] // ranks
 
     def flatten_old():
         for load in loads[1:]:
             load.wait()
 
         def scale_row(r, carry):
-            wide_ref[pl.ds(r * count, count), :] = strength_ref[r] * old_ref[r].astype(jnp.float32)
+            wide_ref[pl.ds(r * pitch, count), :] = strength_ref[r] * old_ref[r].astype(jnp.float32)
             return carry
 
         lax.fori_loop(0, modes, scale_row, 0, unroll=8)
 
     def flatten_snapshots():
         def copy_row(r, carry):
-            wide_ref[pl.ds((r + modes) * count, count), :] = snap_ref[r].astype(jnp.float32)
+            wide_ref[pl.ds((r + modes) * pitch, count), :] = snap_ref[r].astype(jnp.float32)
             return carry
 
         lax.fori_loop(0, snap_ref.shape[0], copy_row, 0, unroll=7)
-        wide_ref[pl.ds((ranks - 1) * count, count), :] = jnp.zeros((count, nx), jnp.float32)
+        wide_ref[pl.ds((ranks - 1) * pitch, count), :] = jnp.zeros((count, nx), jnp.float32)
         take_columns(0, count // 2)
 
     def take_columns(first, stop):
         for b in range(first, stop):
-            column = wide_ref[pl.ds(b, ranks, stride=count), :]
+            column = wide_ref[pl.ds(b, ranks, stride=pitch), :]
             earlier_ref[:, b * nx : (b + 1) * nx] = column.astype(jnp.bfloat16)
 
     def begin_gram():
@@ -397,6 +398,7 @@
     field_ref, level_ref, weights_ref, whole_ref, wide_ref, basis_ref, pass_sem, load_sem, store_sem,
 ):
     ranks, count, nx = basis_ref.shape
+    pitch = wide_ref.shape[0] // ranks
     parts = load_sem.shape[0] - 1
     width = count // parts * nx
     loads = [pltpu.make_async_copy(weights_in, weights_ref, load_sem.at[parts])]
@@ -421,8 +423,8 @@
             pair = jnp.dot(
                 weights, whole_ref[:, b * nx : (b + 2) * nx], preferred_element_type=jnp.float32
             )
-            wide_ref[pl.ds(b, ranks, stride=count), :] = pair[:, :nx]
-            wide_ref[pl.ds(b + 1, ranks, stride=count), :] = pair[:, nx:]
+            wide_ref[pl.ds(b, ranks, stride=pitch), :] = pair[:, :nx]
+            wide_ref[pl.ds(b + 1, ranks, stride=pitch), :] = pair[:, nx:]
     for arrival, copy in zip(arrivals, passes):
         arrival.wait()
         copy.start()
@@ -431,8 +433,8 @@
     stores = []
     for p in range(pieces):
         rows = pl.ds(p * depth, depth)
-        piece = wide_ref[pl.ds(p * depth * count, depth * count), :].astype(jnp.bfloat16)
-        basis_ref[rows] = piece.reshape(depth, count, nx)
+        piece = wide_ref[pl.ds(p * depth * pitch, depth * pitch), :].reshape(depth, pitch, nx)
+        basis_ref[rows] = piece[:, :count].astype(jnp.bfloat16)
         stores.append(pltpu.make_async_copy(basis_ref.at[rows], basis_out.at[rows], store_sem.at[p]))
         stores[-1].start()
     for copy in passes + stores:
@@ -449,6 +451,7 @@
     comps, ny, nz, nx = velocity.shape
     count = comps * (ny // 2) * (nz // 2)
     length = count * nx
+    pitch = count + 8
     share = ranks // n_plane
     assert share * n_plane == ranks
     everyone = n_plane * n_gz
@@ -480,7 +483,7 @@
             pltpu.SMEM((modes,), f32),
             pltpu.VMEM((modes, count, nx), jnp.bfloat16),
             pltpu.VMEM((earlier_count, count, nx), jnp.bfloat16),
-            pltpu.VMEM((ranks * count, nx), f32),
+            pltpu.VMEM((ranks * pitch, nx), f32),
             dma((4,)),
             pltpu.VMEM((3, comps * ny * nz, nx), f32),
             pltpu.VMEM((STAGES,) + velocity.shape, f32),
@@ -525,7 +528,7 @@
             pltpu.VMEM((ranks, ranks), f32),
             pltpu.VMEM((ranks, ranks), jnp.bfloat16),
             pltpu.VMEM((ranks, length), jnp.bfloat16),
-            pltpu.VMEM((ranks * count, nx), f32),
+            pltpu.VMEM((ranks * pitch, nx), f32),
             pltpu.VMEM((ranks, count, nx), jnp.bfloat16),
             dma((4,)),
             dma((5,)),

time: 43.2 us -> 42.9 us (level)
  no operation moved by 1% of the time
where the time goes in v7:
time: 42.9 us; the launch traced here: 42.7 us
  Pallas kernels  42.1 us (98%)
  between operations  0.64 us (1%)
    pallas_call x1, Pallas kernels, local(): pl.pallas_call(functools.partial(kernel, sizes, float(length * n_plane *...  38.7 us
    pallas_call x1, Pallas kernels, local(): pl.pallas_call(rotate, out_shape=(jax.ShapeDtypeStruct(velocity.shape, f3...  3.39 us

profile of v7, /device:TPU:0, one launch (start us, length us, event | category | flops | bytes accessed | tf_op | source)
XLA Modules:
  0.0 42.7 jit_solution(1383819019524160127)
XLA Ops:
  0.6 38.7 %shard_map.67 = (f32[3,8,8,128]{3,2,1,0:T(8,128)}, f32[128,128]{1,0:T(8,128)}, bf16[128,128]{1,0:T(8,128)(2,1)}, bf16[128,6144]{1,0:T(8,128)(2,1)}) custom-call(f32[3,8,8,128]{3,2,1,0:T(8,128)} %v_hbm.1, f32[64]{0:T(128)} %strength_hbm.1, bf16[64,48,128]{2,1,0:T(8,128)(2,1)} %bitcast.3, bf16[63,48,128]{2,1,0:T(8,128)(2,1)} %bitcast.4), custom_call_target="tpu_custom_call" | custom-call | tf_op jit(solution)/shard_map/pallas_call | solution.py:463
  39.4 3.4 %shard_map.68 = (f32[3,8,8,128]{3,2,1,0:T(8,128)}, f32[128,128]{1,0:T(8,128)}, bf16[128,48,128]{2,1,0:T(8,128)(2,1)}) custom-call(f32[3,8,8,128]{3,2,1,0:T(8,128)} %get-tuple-element.10.field_in, f32[128,128]{1,0:T(8,128)} %get-tuple-element.11.level_in, bf16[128,128]{1,0:T(8,128)(2,1)} %get-tuple-element.12.weights_in, ...), custom_call_target="tpu_custom_call" | custom-call | tf_op jit(solution)/shard_map/pallas_call | solution.py:517
